TPU v7x, 256 devices: a whole 4x4x8 slice. The times are simulated.
256 devices in a mesh: chain: 8 (over x, core), sector: 32 (over z, y).
Axes of the slice: x: 4, y: 4, z: 8, core: 2. Of those that a mesh axis runs over, the one named last changes fastest.
Arguments:
- wavefunction: float32 [8, 128, 24, 384], P('chain', 'sector')
- transfer: float32 [8, 128, 576], P('chain', 'sector')
- left_env: bfloat16 [8, 256, 13, 576], P('chain', 'sector')
- right_env: bfloat16 [8, 256, 13, 576], P('chain', 'sector')
- pair_ops: bfloat16 [8, 13, 256], P('chain')
- env_slot: int32 [8, 128], P('chain'), may hold values from 0 to 255, as said below
- kept_ranks: int32 [8, 128], P('chain', 'sector'), may hold values from 6 to 24
Outputs:
- new_state: float32 [8, 128, 24, 384], P('chain', 'sector')
- energy: float32 [8], P('chain')
Inputs may be any that keep to these rules, and one draw needn't show every extreme that they name: `env_slot`: within a segment the values are distinct; slot g lies at sector index floor(g / 8). The 4 sectors i * 4 to (i + 1) * 4 - 1 have their slots at 4 different indices; in every segment some index holds the slots of 8 sectors.
All inputs are finite; a program needn't handle non-finite values.
Results may differ from a plain program's by a relative error of at most 0.0062.
Values may be sent and summed in bfloat16 or wider, within the bound.
A program may use at most 64 MiB of HBM per device.

v0:
```python
import jax
import jax.numpy as jnp
from jax import lax
from jax.sharding import PartitionSpec as P

ITERS = 4


exact_mode = lax.Precision.HIGHEST


def carried_in(part, axis, combine, identity):
    place = lax.axis_index(axis)
    gathered = lax.all_gather(part, axis)
    state = jnp.zeros_like(part) + jnp.asarray(identity, part.dtype)

    def one(lap, state):
        return combine(state, lax.dynamic_index_in_dim(gathered, lap, 0, False))

    return lax.fori_loop(0, place, one, state)


def apply_terms(state_block, left_terms, right_terms, pair_terms):
    bond_dim = state_block.shape[0]
    term_count = left_terms.shape[0]
    pair_dim = state_block.shape[1] // bond_dim
    state_grid = state_block.reshape(bond_dim, pair_dim, bond_dim)
    pair_mats = pair_terms.reshape(term_count, pair_dim, pair_dim)
    mixed_pair = jnp.einsum(
        "lpr,wqp->wlqr", state_grid, pair_mats, preferred_element_type=jnp.float32
    ).astype(jnp.bfloat16)
    right_mats = right_terms.reshape(term_count, bond_dim, bond_dim)
    moved_right = jnp.einsum(
        "wlqr,wsr->wlqs", mixed_pair, right_mats, preferred_element_type=jnp.float32
    ).astype(jnp.bfloat16)
    left_cat = jnp.transpose(left_terms.reshape(term_count, bond_dim, bond_dim), (1, 0, 2)).reshape(
        bond_dim, term_count * bond_dim
    )
    return jnp.dot(
        left_cat,
        moved_right.reshape(term_count * bond_dim, pair_dim * bond_dim),
        preferred_element_type=jnp.float32,
    )


def lowest_pair(diagonal, offdiag):
    padded = jnp.concatenate(
        [jnp.zeros((1,), jnp.float32), jnp.abs(offdiag), jnp.zeros((1,), jnp.float32)]
    )
    bounds = diagonal - padded[:-1] - padded[1:]
    initial = jnp.min(bounds) - 1.0
    dimension = diagonal.shape[0]

    def newton(unused_index, estimate):
        value_prev = jnp.ones((), jnp.float32)
        value_now = diagonal[0] - estimate
        slope_prev = jnp.zeros((), jnp.float32)
        slope_now = -jnp.ones((), jnp.float32)
        for position in range(1, dimension):
            shifted = diagonal[position] - estimate
            weight = offdiag[position - 1] * offdiag[position - 1]
            value_next = shifted * value_now - weight * value_prev
            slope_next = shifted * slope_now - value_now - weight * slope_prev
            value_prev, value_now = (value_now, value_next)
            slope_prev, slope_now = (slope_now, slope_next)
        return estimate - value_now / slope_now

    energy = lax.fori_loop(0, 40, newton, initial)
    coefficients = [jnp.ones((), jnp.float32), (energy - diagonal[0]) / offdiag[0]]
    for position in range(1, dimension - 1):
        following = (
            (energy - diagonal[position]) * coefficients[position]
            - offdiag[position - 1] * coefficients[position - 1]
        ) / offdiag[position]
        coefficients.append(following)
    stacked = jnp.stack(coefficients)
    return (energy, stacked / jnp.sqrt(jnp.sum(stacked * stacked)))


def body(wavefunction, transfer, left_env, right_env, pair_ops, env_slot, kept_ranks):
    sector_count = lax.axis_size("sector")
    my_index = lax.axis_index("sector")
    local_count = wavefunction.shape[1]
    bond_dim = wavefunction.shape[2]
    column_count = wavefunction.shape[3]
    slot_count = left_env.shape[1]
    steps_here = transfer[0].reshape(local_count, bond_dim, bond_dim)
    identity_blocks = jnp.broadcast_to(jnp.eye(bond_dim, dtype=jnp.float32), steps_here.shape)

    def compose(earlier, latter):
        return jnp.einsum("kij,kjl->kil", latter, earlier, precision=exact_mode)

    prefix = carried_in(steps_here, "chain", compose, identity_blocks)
    slot_all = env_slot[0]
    owner_all = slot_all // slot_count
    within_all = slot_all - owner_all * slot_count
    peer_ids = jnp.arange(sector_count, dtype=jnp.int32)
    owner_mine = lax.dynamic_slice_in_dim(owner_all, my_index * local_count, local_count)
    match_grid = owner_all.reshape(sector_count, local_count) == my_index
    from_home = jnp.any(match_grid, axis=1)
    slot_of_home = jnp.sum(
        jnp.where(match_grid, within_all.reshape(sector_count, local_count), 0), axis=1
    )
    sends_to = owner_mine[:, None] == peer_ids[None, :]
    present = jnp.any(sends_to, axis=0)
    local_ids = jnp.arange(local_count, dtype=jnp.int32)
    picked = jnp.sum(jnp.where(sends_to, local_ids[:, None], 0), axis=0)
    slot_ids = jnp.arange(slot_count, dtype=jnp.int32)
    slot_hits = (slot_of_home[None, :] == slot_ids[:, None]) & from_home[None, :]
    slot_used = jnp.any(slot_hits, axis=1)
    home_of_slot = jnp.sum(jnp.where(slot_hits, peer_ids[None, :], 0), axis=1)
    pair_terms = pair_ops[0]
    left_here = left_env[0]
    right_here = right_env[0]
    batched_terms = jax.vmap(apply_terms, in_axes=(0, 0, 0, None))
    initial = wavefunction[0]
    norm_start = lax.psum(jnp.sum(initial * initial), "sector")
    current = initial / jnp.sqrt(norm_start)
    previous = jnp.zeros_like(current)
    coupling = jnp.zeros((), jnp.float32)
    basis = []
    diagonal = []
    offdiag = []
    for section in range(ITERS):
        basis.append(current)
        image_turned = jnp.einsum("klm,klx->kmx", prefix, current, precision=exact_mode).astype(
            jnp.bfloat16
        )
        outgoing = jnp.where(
            present[:, None, None], image_turned[picked], jnp.zeros((), image_turned.dtype)
        )
        arrived = lax.all_to_all(outgoing, "sector", split_axis=0, concat_axis=0, tiled=True)
        in_slots = jnp.where(
            slot_used[:, None, None], arrived[home_of_slot], jnp.zeros((), arrived.dtype)
        )
        finished = batched_terms(in_slots, left_here, right_here, pair_terms)
        reply = jnp.where(
            from_home[:, None, None], finished[slot_of_home], jnp.zeros((), finished.dtype)
        )
        returned = lax.all_to_all(reply, "sector", split_axis=0, concat_axis=0, tiled=True)
        inner_terms = returned[owner_mine]
        result = jnp.einsum("klm,kmx->klx", prefix, inner_terms, precision=exact_mode)
        correlation = lax.psum(jnp.sum(current * result), "sector")
        diagonal.append(correlation)
        if section + 1 < ITERS:
            result = result - correlation * current - coupling * previous
            coupling = jnp.sqrt(lax.psum(jnp.sum(result * result), "sector"))
            offdiag.append(coupling)
            previous = current
            current = result / coupling
    energy, coefficients = lowest_pair(jnp.stack(diagonal), jnp.stack(offdiag))
    combined = basis[0] * coefficients[0]
    for section in range(1, ITERS):
        combined = combined + coefficients[section] * basis[section]
    right_index = jnp.arange(column_count, dtype=jnp.int32) % bond_dim
    truncated = jnp.where(right_index[None, None, :] < kept_ranks[0][:, None, None], combined, 0.0)
    norm_end = lax.psum(jnp.sum(truncated * truncated), "sector")
    entries = float(local_count * sector_count * bond_dim * column_count)
    new_state = truncated * jnp.sqrt(entries / norm_end)
    return (new_state[None], energy.reshape(1))


def solution(mesh):
    return jax.shard_map(
        body,
        mesh=mesh,
        in_specs=(
            P("chain", "sector", None, None),
            P("chain", "sector", None),
            P("chain", "sector", None, None),
            P("chain", "sector", None, None),
            P("chain", None, None),
            P("chain", None),
            P("chain", "sector"),
        ),
        out_specs=(P("chain", "sector", None, None), P("chain")),
        check_vma=False,
    )
```

profile of v0, /device:TPU:4, one launch (start us, length us, event | category | flops | bytes accessed | tf_op | source)
XLA Modules:
  0.0 1131.9 jit_solution(2864704325556592797)
XLA Ops:
  1.5 13.2 %all_gather.3 = f32[8,4,24,24]{3,2,1,0:T(8,128)S(1)} all-gather(f32[1,4,24,24]{3,2,1,0:T(8,128)S(1)} %all_gather_reshape_squeeze.3), channel_id=1, replica_groups=mesh['chain'=8,'sector'=32] {'chain'}, dimensions={0}, use_global_device_ids=true | all-gather | bytes 82944 | tf_op jit(solution)/shard_map/all_gather | solution.py:14
  16.6 77.2 %psum.63 = f32[]{:T(128)} all-reduce(f32[]{:T(128)} %multiply_reduce_fusion.6), channel_id=1, replica_groups=mesh['chain'=8,'sector'=32] {'sector'}, use_global_device_ids=true, to_apply=%region_1.2 | all-reduce | flops 1 | bytes 8 | tf_op jit(solution)/shard_map/psum | solution.py:117
  104.7 10.5 all-to-all-done
  119.9 5.4 fusion.12
  125.3 11.1 copy.50
  136.4 13.1 %reshape.154 = bf16[8,312,384]{2,1,0:T(8,128)(2,1)S(1)} reshape(bf16[8,13,24,16,24]{4,3,2,1,0:T(8,128)(2,1)} %copy.50) | data formatting | bytes 3833856 | tf_op jit(solution)/shard_map/vmap()/reshape | solution.py:41
  155.9 19.9 %all-to-all-done.1 = f32[32,24,384]{2,1,0:T(8,128)S(1)} async-done(((f32[32,24,384]{2,1,0:T(8,128)}), f32[32,24,384]{2,1,0:T(8,128)S(1)}, u32[]{:S(2)}, u32[]{:S(2)}) %all-to-all-start.1) | async-done | bytes 1179680 | tf_op jit(solution)/shard_map/all_to_all | solution.py:140
  177.3 71.9 %psum.64 = f32[]{:T(128)} all-reduce(f32[]{:T(128)} %get-tuple-element.192), channel_id=1, replica_groups=mesh['chain'=8,'sector'=32] {'sector'}, use_global_device_ids=true, to_apply=%region_11.12 | all-reduce | flops 1 | bytes 8 | tf_op jit(solution)/shard_map/psum | solution.py:143
  250.5 71.0 %psum.65 = f32[]{:T(128)} all-reduce(f32[]{:T(128)} %multiply_reduce_fusion.5), channel_id=1, replica_groups=mesh['chain'=8,'sector'=32] {'sector'}, use_global_device_ids=true, to_apply=%region_13.14 | all-reduce | flops 1 | bytes 8 | tf_op jit(solution)/shard_map/psum | solution.py:147
  324.2 21.3 %all_to_all.40 = bf16[32,24,384]{2,1,0:T(8,128)(2,1)S(1)} all-to-all(bf16[32,24,384]{2,1,0:T(8,128)(2,1)S(1)} %broadcast_select_fusion.6), channel_id=1, replica_groups=mesh['chain'=8,'sector'=32] {'sector'}, dimensions={0} | all-to-all | bytes 1179648 | tf_op jit(solution)/shard_map/all_to_all | solution.py:132
  350.1 5.4 fusion.15
  355.5 11.1 copy.55
  366.6 13.1 %reshape.156 = bf16[8,312,384]{2,1,0:T(8,128)(2,1)S(1)} reshape(bf16[8,13,24,16,24]{4,3,2,1,0:T(8,128)(2,1)} %copy.55) | data formatting | bytes 3833856 | tf_op jit(solution)/shard_map/vmap()/reshape | solution.py:41
  381.0 26.0 %all_to_all.41 = f32[32,24,384]{2,1,0:T(8,128)S(1)} all-to-all(f32[32,24,384]{2,1,0:T(8,128)S(1)} %broadcast_select_fusion.2), channel_id=1, replica_groups=mesh['chain'=8,'sector'=32] {'sector'}, dimensions={0} | all-to-all | bytes 2359296 | tf_op jit(solution)/shard_map/all_to_all | solution.py:140
  408.5 70.9 %psum.66 = f32[]{:T(128)} all-reduce(f32[]{:T(128)} %get-tuple-element.194), channel_id=1, replica_groups=mesh['chain'=8,'sector'=32] {'sector'}, use_global_device_ids=true, to_apply=%region_15.16 | all-reduce | flops 1 | bytes 8 | tf_op jit(solution)/shard_map/psum | solution.py:143
  480.6 73.8 %psum.67 = f32[]{:T(128)} all-reduce(f32[]{:T(128)} %get-tuple-element.182), channel_id=1, replica_groups=mesh['chain'=8,'sector'=32] {'sector'}, use_global_device_ids=true, to_apply=%region_17.18 | all-reduce | flops 1 | bytes 8 | tf_op jit(solution)/shard_map/psum | solution.py:147
  556.4 18.4 %all_to_all.42 = bf16[32,24,384]{2,1,0:T(8,128)(2,1)S(1)} all-to-all(bf16[32,24,384]{2,1,0:T(8,128)(2,1)S(1)} %broadcast_select_fusion.5), channel_id=1, replica_groups=mesh['chain'=8,'sector'=32] {'sector'}, dimensions={0} | all-to-all | bytes 1179648 | tf_op jit(solution)/shard_map/all_to_all | solution.py:132
  579.5 5.4 fusion.18
  584.9 11.1 copy.59
  596.0 13.1 %reshape.157 = bf16[8,312,384]{2,1,0:T(8,128)(2,1)S(1)} reshape(bf16[8,13,24,16,24]{4,3,2,1,0:T(8,128)(2,1)} %copy.59) | data formatting | bytes 3833856 | tf_op jit(solution)/shard_map/vmap()/reshape | solution.py:41
  610.4 26.4 %all_to_all.43 = f32[32,24,384]{2,1,0:T(8,128)S(1)} all-to-all(f32[32,24,384]{2,1,0:T(8,128)S(1)} %broadcast_select_fusion.1), channel_id=1, replica_groups=mesh['chain'=8,'sector'=32] {'sector'}, dimensions={0} | all-to-all | bytes 2359296 | tf_op jit(solution)/shard_map/all_to_all | solution.py:140
  638.5 71.3 %psum.68 = f32[]{:T(128)} all-reduce(f32[]{:T(128)} %get-tuple-element.196), channel_id=1, replica_groups=mesh['chain'=8,'sector'=32] {'sector'}, use_global_device_ids=true, to_apply=%region_19.20 | all-reduce | flops 1 | bytes 8 | tf_op jit(solution)/shard_map/psum | solution.py:143
  711.0 73.2 %psum.69 = f32[]{:T(128)} all-reduce(f32[]{:T(128)} %get-tuple-element.180), channel_id=1, replica_groups=mesh['chain'=8,'sector'=32] {'sector'}, use_global_device_ids=true, to_apply=%region_21.22 | all-reduce | flops 1 | bytes 8 | tf_op jit(solution)/shard_map/psum | solution.py:147
  786.1 23.1 %all_to_all.44 = bf16[32,24,384]{2,1,0:T(8,128)(2,1)S(1)} all-to-all(bf16[32,24,384]{2,1,0:T(8,128)(2,1)S(1)} %broadcast_select_fusion.4), channel_id=1, replica_groups=mesh['chain'=8,'sector'=32] {'sector'}, dimensions={0} | all-to-all | bytes 1179648 | tf_op jit(solution)/shard_map/all_to_all | solution.py:132
  814.0 5.4 fusion.21
  819.4 11.1 copy.63
  830.5 13.1 %reshape.158 = bf16[8,312,384]{2,1,0:T(8,128)(2,1)S(1)} reshape(bf16[8,13,24,16,24]{4,3,2,1,0:T(8,128)(2,1)} %copy.63) | data formatting | bytes 3833856 | tf_op jit(solution)/shard_map/vmap()/reshape | solution.py:41
  845.9 4.6 all-to-all-start.7
  850.6 19.4 %all-to-all-done.7 = f32[32,24,384]{2,1,0:T(8,128)S(1)} async-done(((f32[32,24,384]{2,1,0:T(8,128)}), f32[32,24,384]{2,1,0:T(8,128)S(1)}, u32[]{:S(2)}, u32[]{:S(2)}) %all-to-all-start.7) | async-done | bytes 1179680 | tf_op jit(solution)/shard_map/all_to_all | solution.py:140
  871.6 72.1 %psum.70 = f32[]{:T(128)} all-reduce(f32[]{:T(128)} %fusion.28), channel_id=1, replica_groups=mesh['chain'=8,'sector'=32] {'sector'}, use_global_device_ids=true, to_apply=%region_23.24 | all-reduce | flops 1 | bytes 8 | tf_op jit(solution)/shard_map/psum | solution.py:143
  947.6 104.1 %while.23 = (s32[]{:T(128)}, f32[]{:T(128)}, f32[]{:T(128)}, f32[]{:T(128)}, f32[]{:T(128)}, /*index=5*/f32[]{:T(128)}, f32[]{:T(128)}, f32[]{:T(128)}, f32[]{:T...) while((s32[]{:T(128)}, f32[]{:T(128)}, f32[]{:T(128)}, f32[]{:T(128)}, f32[]{:T(128)}, ...), condition=%wide.region_26.27_spmd, body=%wide.region_25.26_spmd.sunk | while | flops 26 | bytes 413 | solution.py:68
  1058.9 70.3 %psum.71 = f32[]{:T(128)} all-reduce(f32[]{:T(128)} %get-tuple-element.176), channel_id=1, replica_groups=mesh['chain'=8,'sector'=32] {'sector'}, use_global_device_ids=true, to_apply=%region_29.30 | all-reduce | flops 1 | bytes 8 | tf_op jit(solution)/shard_map/psum | solution.py:157
  (127 shorter events, 66.4 us)
Async XLA Ops:
  0.6 15.1 %copy-start = (f32[1,4,24,384]{3,2,1,0:T(8,128)S(1)}, f32[1,4,24,384]{3,2,1,0:T(8,128)}, u32[]{:S(2)}) copy-start(f32[1,4,24,384]{3,2,1,0:T(8,128)} %param.11) | copy-start | bytes 442372
  0.6 15.7 %copy-start.13 = (s32[1,128]{1,0:T(1,128)S(1)}, s32[1,128]{1,0:T(1,128)}, u32[]{:S(2)}) copy-start(s32[1,128]{1,0:T(1,128)} %param.16) | copy-start | bytes 1540
  16.6 307.4 %copy-start.5 = (pred[32]{0:T(512)(128)(4,1)}, pred[32]{0:T(512)(128)(4,1)S(1)}, u32[]{:S(2)}) copy-start(pred[32]{0:T(512)(128)(4,1)S(1)} %fusion.51) | copy-start | bytes 100
  94.6 7.2 copy-start.11
  95.0 7.0 copy-start.1
  95.0 7.5 copy-start.2
  96.6 18.6 %all-to-all-start = ((bf16[32,24,384]{2,1,0:T(8,128)(2,1)}), bf16[32,24,384]{2,1,0:T(8,128)(2,1)S(1)}, u32[]{:S(2)}, u32[]{:S(2)}) async-start(bf16[32,24,384]{2,1,0:T(8,128)(2,1)} %broadcast_select_fusion.7), calls=%async_computation | async-start | bytes 1179648 | tf_op jit(solution)/shard_map/all_to_all | solution.py:132
  104.6 240.9 %copy-start.4 = (s32[1024]{0:T(1024)}, s32[1024]{0:T(1024)S(1)}, u32[]{:S(2)}) copy-start(s32[1024]{0:T(1024)S(1)} %pad_clamp_fusion.2) | copy-start | bytes 12292
  104.7 241.3 %copy-start.8 = (pred[8]{0:T(512)(128)(4,1)}, pred[8]{0:T(512)(128)(4,1)S(1)}, u32[]{:S(2)}) copy-start(pred[8]{0:T(512)(128)(4,1)S(1)} %fusion.50) | copy-start | bytes 28
  151.7 24.1 %all-to-all-start.1 = ((f32[32,24,384]{2,1,0:T(8,128)}), f32[32,24,384]{2,1,0:T(8,128)S(1)}, u32[]{:S(2)}, u32[]{:S(2)}) async-start(f32[32,24,384]{2,1,0:T(8,128)} %broadcast_select_fusion.3), calls=%async_computation.1 | async-start | bytes 2359296 | tf_op jit(solution)/shard_map/all_to_all | solution.py:140
  155.9 251.1 %copy-start.3 = (s32[1024]{0:T(1024)}, s32[1024]{0:T(1024)S(1)}, u32[]{:S(2)}) copy-start(s32[1024]{0:T(1024)S(1)} %pad_clamp_fusion) | copy-start | bytes 12292
  407.0 149.2 %copy-start.6 = (pred[32]{0:T(512)(128)(4,1)S(1)}, pred[32]{0:T(512)(128)(4,1)}, u32[]{:S(2)}) copy-start(pred[32]{0:T(512)(128)(4,1)} %copy-done.5) | copy-start | bytes 100
  555.5 20.0 %copy-start.9 = (pred[8]{0:T(512)(128)(4,1)S(1)}, pred[8]{0:T(512)(128)(4,1)}, u32[]{:S(2)}) copy-start(pred[8]{0:T(512)(128)(4,1)} %copy-done.8) | copy-start | bytes 28
  636.7 149.2 %copy-start.7 = (pred[32]{0:T(512)(128)(4,1)S(1)}, pred[32]{0:T(512)(128)(4,1)}, u32[]{:S(2)}) copy-start(pred[32]{0:T(512)(128)(4,1)} %copy-done.5) | copy-start | bytes 100
  785.3 24.7 %copy-start.10 = (pred[8]{0:T(512)(128)(4,1)S(1)}, pred[8]{0:T(512)(128)(4,1)}, u32[]{:S(2)}) copy-start(pred[8]{0:T(512)(128)(4,1)} %copy-done.8) | copy-start | bytes 28
  844.7 5.8 copy-start.12
  845.9 24.2 %all-to-all-start.7 = ((f32[32,24,384]{2,1,0:T(8,128)}), f32[32,24,384]{2,1,0:T(8,128)S(1)}, u32[]{:S(2)}, u32[]{:S(2)}) async-start(f32[32,24,384]{2,1,0:T(8,128)} %broadcast_select_fusion), calls=%async_computation.7 | async-start | bytes 2359296 | tf_op jit(solution)/shard_map/all_to_all | solution.py:140
where the time goes:
time: 1150 us; the launch traced here: 1130 us
  blocking collectives  780 us (68%)
  local copies, waits for them, and re-layouts  116 us (10%)
  loops' own time  104 us (9%)
  waiting for transfers between devices  49.7 us (4%)
  matrix products  40.9 us (4%)
  other arithmetic  18.9 us (2%)
  starting transfers between devices  12.6 us (1%)
    psum x4, blocking collectives, body(): correlation = lax.psum(jnp.sum(current * result), 'sector')  286 us
    psum x3, blocking collectives, body(): coupling = jnp.sqrt(lax.psum(jnp.sum(result * result), 'sector'))  218 us
    another operation x1, loops' own time, lowest_pair(): energy = lax.fori_loop(0, 40, newton, initial)  104 us
    psum x1, blocking collectives, body(): norm_start = lax.psum(jnp.sum(initial * initial), 'sector')  77.2 us
    psum x1, blocking collectives, body(): norm_end = lax.psum(jnp.sum(truncated * truncated), 'sector')  70.3 us
    all_to_all x3, blocking collectives, body(): lax.all_to_all(outgoing, 'sector', split_axis=0, concat_axis=0, tiled=True)  62.8 us
    reshape x4, local copies, waits for them, and re-layouts, apply_terms(): moved_right.reshape(term_count * bond_dim, pair_dim * bond_dim)  52.6 us
    all_to_all x2, blocking collectives, body(): lax.all_to_all(reply, 'sector', split_axis=0, concat_axis=0, tiled=True)  52.4 us
  transfers between devices with their start and end apart: 3, of which 3 were waited for; matrix products, arithmetic and copies ran while one was open for 0% of the time, Pallas kernels for 0%

commit v1 on v0

v1 whole, which is shorter than its diff:
```python
import functools
import jax, jax.numpy as jnp
from jax import lax
from jax.experimental import pallas as pl
from jax.sharding import PartitionSpec as P
from jax.experimental.pallas import tpu as pltpu
F=jnp.float32; H=jnp.bfloat16
NT=4; NB=24; NP=16; NW=13

def split(x):
    h=x.astype(H)
    return h,(x-h.astype(F)).astype(H)

def grab(ref_cols, off, t, lane):
    c0,o=off//128,off%128
    sh=(32*t-o)%128
    a=ref_cols(c0)
    a=pltpu.roll(a,sh,1) if sh else a
    if o+24>128:
        b=ref_cols(c0+1)
        b=pltpu.roll(b,sh,1) if sh else b
        a=jnp.where(lane<32*t+128-o,a,b)
    return jnp.where((lane>=32*t)&(lane<32*t+24),a,0.0)

def full(x):
    return jnp.sum(jnp.sum(x,axis=0,keepdims=True),axis=1,keepdims=True)

def k2(chain_ref,kept_ref,trans_ref,env_ref,x_ref,b_ref,v_ref,st_ref,
       tpad,tbd,ebd,b2,c2,mixed,moved,acat):
    me=chain_ref[0]
    lane=lax.broadcasted_iota(jnp.int32,(1,128),1)
    row128=lax.broadcasted_iota(jnp.int32,(128,128),0)
    col128=lax.broadcasted_iota(jnp.int32,(128,128),1)
    tbd[...]=jnp.zeros_like(tbd)
    for t in range(NT):
        tpad[:,:576]=trans_ref[:,t,:]
        for i in range(NB):
            tbd[pl.ds(32*t+i,8,stride=128),:]=grab(lambda c:tpad[:,c*128:(c+1)*128],24*i,t,lane)
    eye=(row128==col128).astype(F)
    T=[jnp.where(me>c,tbd[c*128:(c+1)*128,:],eye) for c in range(7)]
    mm=lambda a,b: jnp.dot(a,b,precision=lax.Precision.HIGHEST,preferred_element_type=F)
    pre=mm(mm(T[6],mm(T[5],T[4])),mm(mm(T[3],T[2]),mm(T[1],T[0])))
    PT=pre.T
    ph,plo=split(PT)
    bf=b_ref[...].astype(F)
    for q in range(NP):
        off=16*q
        a=bf[:,(off//128)*128:(off//128)*128+128]
        sh=(-(off%128))%128
        a=pltpu.roll(a,sh,1) if sh else a
        tpadb=jnp.where(lane<16,a,0.0)
        tbd[pl.ds(q,13,stride=16),:]=tpadb
    bb=tbd[0:208,:]
    bb=jnp.where(lane<16,bb,0.0)+pltpu.roll(bb,16,1)
    b2[...]=bb[:,:32].astype(H)
    for side in (1,0):
        ebd[...]=jnp.zeros_like(ebd)
        for t in range(NT):
            ev=env_ref[t].astype(F)
            for i in range(NB):
                ebd[pl.ds(32*t+i,13,stride=128),:]=grab(lambda c:ev[:,c*128:(c+1)*128],576*side+24*i,t,lane)
        if side==1:
            for w in range(NW):
                ct=ebd[w*128:(w+1)*128,:].T.astype(H)
                c2[w,0:128,:]=ct
                c2[w,128:256,:]=ct
        else:
            pp=jnp.concatenate([ph,plo],0)
            pq=jnp.concatenate([ph,plo,ph],0)
            for w in range(NW):
                e=ebd[w*128:(w+1)*128,:].astype(H)
                s=jnp.dot(jnp.concatenate([e,e],1),pp,preferred_element_type=F)
                sh,sl=split(s.T)
                at=jnp.dot(jnp.concatenate([sh,sh,sl],1),pq,preferred_element_type=F)
                acat[24*w:24*w+24,:]=at[0:24]+at[32:56]+at[64:88]+at[96:120]
    acat[312:384,:]=jnp.zeros((72,128),F)
    al=acat[...].T
    al=jnp.concatenate([al[32*t:32*t+24] for t in range(NT)],0)[:,:312].astype(H)
    a2=jnp.concatenate([al.astype(F),al.astype(F)],1).astype(H)
    for p in range(NP):
        acc=jnp.zeros((24,128),F)
        for t in range(NT):
            acc=acc+grab(lambda c:x_ref[t,:,c*128:(c+1)*128],24*p,t,lane)
        v_ref[0,pl.ds(p,24,stride=16),:]=acc
    x=v_ref[0]
    n0=jnp.sqrt(full(x*x))
    inv=lambda n: jnp.where(n>0,1.0/n,0.0)
    v_ref[0]=x*inv(n0)
    bm=b2[...]
    tl=lane//32
    alphas=[];betas=[]
    for k in range(4):
        for l in range(0,NB,2):
            xx=jnp.concatenate([v_ref[k,16*l:16*l+16,:],v_ref[k,16*l+16:16*l+32,:]],1)
            h,lo=split(xx)
            o=jnp.dot(bm,jnp.concatenate([h,lo],0),preferred_element_type=F)
            h,lo=split(o)
            mixed[0,l]=h[:,:128]; mixed[0,l+1]=h[:,128:]
            mixed[1,l]=lo[:,:128]; mixed[1,l+1]=lo[:,128:]
        for w in range(NW):
            h=mixed[0,:,16*w:16*w+16,:].reshape(384,128)
            lo=mixed[1,:,16*w:16*w+16,:].reshape(384,128)
            moved[w]=jnp.dot(jnp.concatenate([h,lo],1),c2[w],preferred_element_type=F)
        for q in range(0,NP,2):
            r=jnp.concatenate([jnp.concatenate([moved[w,pl.ds(q+j,24,stride=16),:] for w in range(NW)],0) for j in range(2)],1)
            h=r.astype(H).astype(F)
            o=jnp.dot(a2,jnp.concatenate([h,r-h],0).astype(H),preferred_element_type=F)
            for j in range(2):
                oj=o[:,128*j:128*j+128]
                y=jnp.where(tl==0,oj[0:24],jnp.where(tl==1,oj[24:48],jnp.where(tl==2,oj[48:72],oj[72:96])))
                v_ref[k+1,pl.ds(q+j,24,stride=16),:]=y
        w_=v_ref[k+1]
        if k<3:
            a=full(v_ref[k]*w_)
            r=w_-a*v_ref[k]
            if k>0: r=r-betas[-1]*v_ref[k-1]
            b=jnp.sqrt(full(r*r))
            alphas.append(a); betas.append(b)
            v_ref[k+1]=r*inv(b)
    rows=[]
    for i in range(4):
        for j in range(i,5):
            rows.append(jnp.sum(v_ref[i]*v_ref[j],axis=0,keepdims=True))
    rows+= [jnp.zeros((1,128),F)]*2
    g=jnp.concatenate(rows,0)
    kp=jnp.where(tl==0,kept_ref[0,0],jnp.where(tl==1,kept_ref[0,1],jnp.where(tl==2,kept_ref[0,2],kept_ref[0,3])))
    msk=((lane%32)<kp).astype(F)
    r8=lax.broadcasted_iota(jnp.int32,(8,128),0)
    lhs=jnp.where(r8==0,1.0,jnp.where(r8==1,jnp.broadcast_to(msk,(8,128)),0.0))
    g=jnp.concatenate([g,jnp.zeros((112,128),F)],0)
    s=lax.dot_general(lhs,g,(((1,),(1,)),((),())),precision=lax.Precision.HIGHEST,preferred_element_type=F)
    for i,val in enumerate([n0]+alphas+betas):
        s=s+jnp.where((lane==16+i)&(r8==0),val,0.0)
    st_ref[...]=s

def call_k2(chain,kept,trans,env,x,b):
    return pl.pallas_call(k2,
      out_shape=(jax.ShapeDtypeStruct((5,384,128),F),jax.ShapeDtypeStruct((8,128),F)),
      in_specs=[pl.BlockSpec(memory_space=pltpu.SMEM)]*2+[pl.BlockSpec(memory_space=pltpu.VMEM)]*4,
      out_specs=(pl.BlockSpec(memory_space=pltpu.VMEM),)*2,
      scratch_shapes=[pltpu.VMEM((8,640),F),pltpu.VMEM((1024,128),F),pltpu.VMEM((1664,128),F),
        pltpu.VMEM((208,32),H),pltpu.VMEM((13,256,128),H),pltpu.VMEM((2,24,208,128),H),
        pltpu.VMEM((13,384,128),F),pltpu.VMEM((384,128),F)],
      compiler_params=pltpu.CompilerParams(vmem_limit_bytes=48*2**20),
      name="lanczos_local")(chain,kept,trans,env,x,b)

def global_solve(q0,q1,entries):
    tot=lambda x: jnp.sum(x,axis=1,keepdims=True)
    pos={}
    n=0
    for i in range(4):
        for j in range(i,5):
            pos[i,j]=n; n+=1
    M=[[q0(pos[min(i,j),max(i,j)]) for j in range(4)] for i in range(4)]
    Mk=[[q1(pos[min(i,j),max(i,j)]) for j in range(4)] for i in range(4)]
    Wv=[q0(pos[i,4]) for i in range(4)]
    n0=q0(16); al=[q0(17+i) for i in range(3)]; be=[q0(20+i) for i in range(3)]
    def tmul(c):
        k=len(c)-1
        y=[None]*min(k+2,4)
        def add(i,z):
            y[i]=z if y[i] is None else y[i]+z
        for j in range(min(k+1,3)):
            add(j,al[j]*c[j]); add(j+1,be[j]*c[j])
            if j>0: add(j-1,be[j-1]*c[j])
        return y
    def dot(Mx,a,b):
        acc=None
        for i in range(len(a)):
            s=None
            for j in range(len(b)):
                z=Mx[i][j]*b[j]; s=z if s is None else s+z
            s=s*a[i]; acc=s if acc is None else acc+s
        return acc
    c=[n0/jnp.sqrt(tot(n0*n0))]
    cp=[]; b=None
    cs=[]; A=[]; Bt=[]
    for k in range(4):
        cs.append(c)
        y=tmul(c)
        g=dot(M,c,y)
        if k==3:
            s=None
            for i in range(4):
                z=c[i]*Wv[i]; s=z if s is None else s+z
            g=g+s*c[3]
        a=tot(g); A.append(a)
        if k<3:
            r=[]
            for i in range(len(y)):
                z=y[i]
                if i<len(c): z=z-a*c[i]
                if i<len(cp): z=z-b*cp[i]
                r.append(z)
            b=jnp.sqrt(tot(dot(M,r,r))); Bt.append(b)
            cp=c; c=[z/b for z in r]
    ab=[jnp.abs(z) for z in Bt]
    bounds=[A[0]-ab[0],A[1]-ab[0]-ab[1],A[2]-ab[1]-ab[2],A[3]-ab[2]]
    init=jnp.minimum(jnp.minimum(bounds[0],bounds[1]),jnp.minimum(bounds[2],bounds[3]))-1.0
    B2=[z*z for z in Bt]
    def newton(_,e):
        vp=jnp.ones_like(e); vn=A[0]-e; sp=jnp.zeros_like(e); sn=-jnp.ones_like(e)
        for p in range(1,4):
            sh=A[p]-e; w=B2[p-1]
            v2=sh*vn-w*vp; s2=sh*sn-vn-w*sp
            vp,vn=vn,v2; sp,sn=sn,s2
        return e-vn/sn
    e=lax.fori_loop(0,40,newton,init)
    co=[jnp.ones_like(e),(e-A[0])/Bt[0]]
    for p in range(1,3):
        co.append(((e-A[p])*co[p]-Bt[p-1]*co[p-1])/Bt[p])
    nrm=jnp.sqrt(co[0]*co[0]+co[1]*co[1]+co[2]*co[2]+co[3]*co[3])
    f=[None]*4
    for k in range(4):
        for i in range(len(cs[k])):
            z=(co[k]/nrm)*cs[k][i]; f[i]=z if f[i] is None else f[i]+z
    scale=jnp.sqrt(entries/tot(dot(Mk,f,f)))
    return e,[z*scale for z in f]

def k4(entries,me_ref,kept_ref,st_ref,v_ref,out_ref,en_ref,ybuf):
    me=me_ref[0]
    lane=lax.broadcasted_iota(jnp.int32,(1,128),1)
    z=jnp.zeros((96,128),F)
    Q0=jnp.concatenate([st_ref[:,0,:],z],0).T
    Q1=jnp.concatenate([st_ref[:,1,:],z],0).T
    e,f=global_solve(lambda i:Q0[i:i+1,:],lambda i:Q1[i:i+1,:],entries)
    en_ref[...]=jnp.broadcast_to(e,(8,128))
    tl=lane//32
    kp=jnp.where(tl==0,kept_ref[0,0],jnp.where(tl==1,kept_ref[0,1],jnp.where(tl==2,kept_ref[0,2],kept_ref[0,3])))
    keep=(lane%32)<kp
    mine=[jnp.sum(jnp.where(lane==me,z,0.0),axis=1,keepdims=True) for z in f]
    y=mine[0]*v_ref[0]
    for i in range(1,4): y=y+mine[i]*v_ref[i]
    ybuf[...]=jnp.where(keep,y,0.0)
    for p in range(NP):
        a=ybuf[pl.ds(p,24,stride=16),:]
        for t in range(NT):
            out_ref[t,:,24*p:24*p+24]=a[:,32*t:32*t+24]

def call_k4(entries,me,kept,st,v):
    return pl.pallas_call(functools.partial(k4,entries),
      out_shape=(jax.ShapeDtypeStruct((4,24,384),F),jax.ShapeDtypeStruct((8,128),F)),
      in_specs=[pl.BlockSpec(memory_space=pltpu.SMEM)]*2+[pl.BlockSpec(memory_space=pltpu.VMEM)]*2,
      out_specs=(pl.BlockSpec(memory_space=pltpu.VMEM),)*2,
      scratch_shapes=[pltpu.VMEM((384,128),F)],
      compiler_params=pltpu.CompilerParams(vmem_limit_bytes=16*2**20),
      name="global_solve")(me,kept,st,v)

def body(wavefunction, transfer, left_env, right_env, pair_ops, env_slot, kept_ranks):
    sector_count = lax.axis_size("sector")
    me = lax.axis_index("sector")
    chain = lax.axis_index("chain")
    slots = left_env.shape[1]
    trans = lax.all_gather(transfer[0], "chain")
    slot_all = env_slot[0]
    owner = slot_all // slots
    within = slot_all - owner * slots
    match = owner.reshape(sector_count, NT) == me
    slot_of_home = jnp.sum(jnp.where(match, within.reshape(sector_count, NT), 0), axis=1)
    env = jnp.concatenate([left_env[0], right_env[0]], axis=-1)
    arrived = lax.all_to_all(env[slot_of_home], "sector", split_axis=0, concat_axis=0, tiled=True)
    owner_mine = lax.dynamic_slice_in_dim(owner, me * NT, NT)
    mine = arrived[owner_mine]
    v, st = call_k2(chain.reshape(1), kept_ranks, trans, mine, wavefunction[0], pair_ops[0])
    stats = lax.all_gather(st, "sector")
    entries = float(sector_count * NT * NB * NP * NB)
    out, en = call_k4(entries, me.reshape(1), kept_ranks, stats, v)
    return out[None], en[0, :1]


def solution(mesh):
    return jax.shard_map(
        body,
        mesh=mesh,
        in_specs=(
            P("chain", "sector", None, None),
            P("chain", "sector", None),
            P("chain", "sector", None, None),
            P("chain", "sector", None, None),
            P("chain", None, None),
            P("chain", None),
            P("chain", "sector"),
        ),
        out_specs=(P("chain", "sector", None, None), P("chain")),
        check_vma=False,
    )
```

time: 1150 us -> 112 us (0.10); the launches traced: 1130 us -> 112 us
  blocking collectives: 780 us -> 54.5 us
  local copies, waits for them, and re-layouts: 116 us -> 4.41 us
  loops' own time: 104 us -> 0 us
  matrix products: 40.9 us -> 0 us
  waiting for transfers between devices: 49.7 us -> 19.1 us
  Pallas kernels: 0 us -> 19.6 us
  other arithmetic: 18.9 us -> 1.67 us
    psum x9 -> x0, blocking collectives: 652 us -> none  [the longest x4 286 us: body(): correlation = lax.psum(jnp.sum(current * result), 'sector')]
    all_to_all x5 -> x0, blocking collectives: 115 us -> none  [the longest x3 62.8 us: body(): lax.all_to_all(outgoing, 'sector', split_axis=0, concat_axis=0, tiled=True)]
    another operation x2 -> x0, loops' own time: 104 us -> none  [the longest x1 104 us: lowest_pair(): energy = lax.fori_loop(0, 40, newton, initial)]
    reshape x5 -> x0, local copies, waits for them, and re-layouts: 53.3 us -> none  [the longest x4 52.6 us: apply_terms(): moved_right.reshape(term_count * bond_dim, pair_dim * bond_dim)]
    convert_element_type x4 -> x0, local copies, waits for them, and re-layouts: 44.4 us -> none  [apply_terms(): moved_right = jnp.einsum('wlqr,wsr->wlqs', mixed_pair, right_mats, prefer...]
    all_gather x1 -> x2, blocking collectives: 13.2 us -> 54.5 us  [the longest x1 43 us: body(): stats = lax.all_gather(st, 'sector')]
    dot_general x24 -> x0, matrix products: 40.9 us -> none  [the longest x4 21.5 us: apply_terms(): jnp.einsum('wlqr,wsr->wlqs', mixed_pair, right_mats, preferred_element_ty...]
    all_to_all x3 -> x1, waiting for transfers between devices: 49.7 us -> 19.1 us  [body(): lax.all_to_all(env[slot_of_home], 'sector', split_axis=0, concat_axis=0,...]
  transfers between devices with their start and end apart: 3 -> 1, of which waited for: 3 -> 1; matrix products, arithmetic and copies ran while one was open for 0% -> 0% of each run, Pallas kernels for 0% -> 0%
where the time goes in v1:
time: 112 us
  blocking collectives  54.5 us (49%)
  Pallas kernels  19.6 us (18%)
  waiting for transfers between devices  19.1 us (17%)
  starting transfers between devices  11.6 us (10%)
  local copies, waits for them, and re-layouts  4.41 us (4%)
  other arithmetic  1.67 us (1%)
    all_gather x1, blocking collectives, body(): stats = lax.all_gather(st, 'sector')  43 us
    all_to_all x1, waiting for transfers between devices, body(): lax.all_to_all(env[slot_of_home], 'sector', split_axis=0, concat_axis=0,...  19.1 us
    pallas_call x1, Pallas kernels, call_k2(): pl.pallas_call(k2, out_shape=(jax.ShapeDtypeStruct((5, 384, 128), F), jax...  16.3 us
    all_to_all x1, starting transfers between devices, body(): lax.all_to_all(env[slot_of_home], 'sector', split_axis=0, concat_axis=0,...  11.6 us
    all_gather x1, blocking collectives, body(): trans = lax.all_gather(transfer[0], 'chain')  11.5 us
    pallas_call x1, Pallas kernels, call_k4(): pl.pallas_call(functools.partial(k4, entries), out_shape=(jax.ShapeDtypeS...  3.34 us
  transfers between devices with their start and end apart: 1, of which 1 were waited for; matrix products, arithmetic and copies ran while one was open for 0% of the time, Pallas kernels for 0%

profile of v1, /device:TPU:4, one launch (start us, length us, event | category | flops | bytes accessed | tf_op | source)
XLA Modules:
  0.0 111.7 jit_solution(17556850132534068278)
XLA Ops:
  0.6 0.5 broadcast.107
  1.1 1.3 %reduce.3 = s32[128]{0:T(128)S(1)} reduce(s32[1,128]{1,0:T(1,128)} %param.12, s32[]{:T(128)} %broadcast.107), dimensions={0}, to_apply=%param.12.reduce_sub_computation.3 | reduce | bytes 1028 | tf_op args[5]
  2.5 0.1 squeeze.22
  2.6 0.1 select_reduce_fusion
  2.7 1.0 copy_bitcast_fusion
  3.7 0.1 pad_maximum_fusion
  3.8 1.7 %gather_fusion = bf16[32,13,1152]{2,1,0:T(8,128)(2,1)} fusion(bf16[8,13,1152]{2,1,0:T(8,128)(2,1)S(1)} %pad_maximum_fusion, s32[1024]{0:T(1024)S(1)} %pad_clamp_fusion.1), kind=kCustom, calls=%fused_computation | custom fusion | bytes 1917056 | tf_op jit(solution)/shard_map/gather | solution.py:261
  5.5 0.0 copy-start.3
  5.5 0.0 copy-start.4
  5.5 0.0 copy-start
  5.5 0.0 copy-start.1
  5.6 0.0 copy-start.2
  5.6 11.6 %all-to-all-start = ((bf16[32,13,1152]{2,1,0:T(8,128)(2,1)}), bf16[32,13,1152]{2,1,0:T(8,128)(2,1)S(1)}, u32[]{:S(2)}, u32[]{:S(2)}) async-start(bf16[32,13,1152]{2,1,0:T(8,128)(2,1)} %gather_fusion), calls=%async_computation | async-start | bytes 2359296 | tf_op jit(solution)/shard_map/all_to_all | solution.py:261
  17.2 0.0 copy-done.3
  17.2 11.5 %all_gather.9.trans_ref = f32[8,4,576]{2,1,0:T(4,128)S(1)} all-gather(f32[1,4,576]{2,1,0:T(4,128)S(1)} %copy-done.3), channel_id=1, replica_groups=mesh['chain'=8,'sector'=32] {'chain'}, dimensions={0}, use_global_device_ids=true | all-gather | bytes 82944 | tf_op jit(solution)/shard_map/all_gather | solution.py:254
  28.8 0.0 copy-done.4
  28.8 0.1 compare_select_fusion
  28.9 19.1 %all-to-all-done = bf16[32,13,1152]{2,1,0:T(8,128)(2,1)S(1)} async-done(((bf16[32,13,1152]{2,1,0:T(8,128)(2,1)}), bf16[32,13,1152]{2,1,0:T(8,128)(2,1)S(1)}, u32[]{:S(2)}, u32[]{:S(2)}) %all-to-all-start) | async-done | bytes 958496 | tf_op jit(solution)/shard_map/all_to_all | solution.py:261
  48.0 0.6 gather_fusion.1
  48.6 0.0 copy-done
  48.6 0.0 copy-done.1
  48.6 0.0 copy-done.2
  48.6 16.3 %lanczos_local.1 = (f32[5,384,128]{2,1,0:T(8,128)S(1)}, f32[8,128]{1,0:T(8,128)S(1)}) custom-call(s32[1]{0:T(128)} %bitcast.1.chain_ref, s32[1,4]{1,0:T(1,128)S(1)} %copy-done.2, f32[8,4,576]{2,1,0:T(4,128)S(1)} %all_gather.9.trans_ref, bf16[4,13,1152]{2,1,0:T(8,128)(2,1)S(1)} %gather_fusion.1, f32[4,24,384]{2,1,0:T(8,128)S(1)} %bitcast.24, ...), custom_call_target="tpu_custom_call" | custom-call | tf_op jit(solution)/shard_map/lanczos_local/pallas_call | solution.py:137
  64.9 43.0 %all-gather = f32[256,128]{1,0:T(8,128)S(1)} all-gather(f32[8,128]{1,0:T(8,128)S(1)} %get-tuple-element.6), channel_id=2, replica_groups=mesh['chain'=8,'sector'=32] {'sector'}, dimensions={0}, use_global_device_ids=true | all-gather | bytes 135168 | tf_op jit(solution)/shard_map/all_gather | solution.py:265
  107.9 3.3 %global_solve.1 = (f32[4,24,384]{2,1,0:T(8,128)}, f32[8,128]{1,0:T(8,128)S(1)}) custom-call(s32[1]{0:T(128)} %bitcast.me_ref, s32[1,4]{1,0:T(1,128)S(1)} %copy-done.2, f32[32,8,128]{2,1,0:T(8,128)S(1)} %bitcast.23, f32[5,384,128]{2,1,0:T(8,128)S(1)} %get-tuple-element.7.v_ref), custom_call_target="tpu_custom_call" | custom-call | tf_op jit(solution)/shard_map/global_solve/pallas_call | solution.py:241
  111.2 0.5 slice.3
  (4 shorter events, 0.0 us)
Async XLA Ops:
  5.5 11.7 %copy-start.3 = (f32[1,4,576]{2,1,0:T(4,128)S(1)}, f32[1,4,576]{2,1,0:T(4,128)}, u32[]{:S(2)}) copy-start(f32[1,4,576]{2,1,0:T(4,128)} %param.8) | copy-start | bytes 27652
  5.5 23.2 %copy-start.4 = (s32[1,128]{1,0:T(1,128)S(1)}, s32[1,128]{1,0:T(1,128)}, u32[]{:S(2)}) copy-start(s32[1,128]{1,0:T(1,128)} %param.12) | copy-start | bytes 1540
  5.5 43.0 %copy-start = (f32[1,4,24,384]{3,2,1,0:T(8,128)S(1)}, f32[1,4,24,384]{3,2,1,0:T(8,128)}, u32[]{:S(2)}) copy-start(f32[1,4,24,384]{3,2,1,0:T(8,128)} %param.7) | copy-start | bytes 442372
  5.5 43.0 %copy-start.1 = (bf16[1,13,256]{2,1,0:T(8,128)(2,1)S(1)}, bf16[1,13,256]{2,1,0:T(8,128)(2,1)}, u32[]{:S(2)}) copy-start(bf16[1,13,256]{2,1,0:T(8,128)(2,1)} %param.11) | copy-start | bytes 19972
  5.6 43.1 %copy-start.2 = (s32[1,4]{1,0:T(1,128)S(1)}, s32[1,4]{1,0:T(1,128)}, u32[]{:S(2)}) copy-start(s32[1,4]{1,0:T(1,128)} %kept_ref.3) | copy-start | bytes 52
  5.6 42.4 %all-to-all-start = ((bf16[32,13,1152]{2,1,0:T(8,128)(2,1)}), bf16[32,13,1152]{2,1,0:T(8,128)(2,1)S(1)}, u32[]{:S(2)}, u32[]{:S(2)}) async-start(bf16[32,13,1152]{2,1,0:T(8,128)(2,1)} %gather_fusion), calls=%async_computation | async-start | bytes 2359296 | tf_op jit(solution)/shard_map/all_to_all | solution.py:261

commit v2 on v1

--- a/solution.py
+++ b/solution.py
@@ -58,7 +58,7 @@
         for t in range(NT):
             ev=env_ref[t].astype(F)
             for i in range(NB):
-                ebd[pl.ds(32*t+i,13,stride=128),:]=grab(lambda c:ev[:,c*128:(c+1)*128],576*side+24*i,t,lane)
+                ebd[pl.ds(32*t+i,13,stride=128),:]=grab(lambda c:ev[:,c*128:(c+1)*128],576*side+24*i,t,lane)[:13]
         if side==1:
             for w in range(NW):
                 ct=ebd[w*128:(w+1)*128,:].T.astype(H)
@@ -217,10 +217,82 @@
     scale=jnp.sqrt(entries/tot(dot(Mk,f,f)))
     return e,[z*scale for z in f]
 
-def k4(entries,me_ref,kept_ref,st_ref,v_ref,out_ref,en_ref,ybuf):
-    me=me_ref[0]
+
+def device_id(ch, sec):
+    return (ch, sec)
+
+def exchange(nsec,nch,left,right,slot_ref,tr,env_out,trans_out,cat,stage,recv,trecv,ssem,rsem,tssem,trsem):
+    me=lax.axis_index("sector"); ch=lax.axis_index("chain")
+    cap=left.shape[0]
+    bar=pltpu.get_barrier_semaphore()
+    def sig(j,c):
+        pl.semaphore_signal(bar,inc=1,device_id=(ch,lax.rem(me+j,nsec)),device_id_type=pl.DeviceIdType.MESH)
+        return c
+    lax.fori_loop(1,nsec,sig,0)
+    def sigc(j,c):
+        pl.semaphore_signal(bar,inc=1,device_id=(lax.rem(ch+j,nch),me),device_id_type=pl.DeviceIdType.MESH)
+        return c
+    lax.fori_loop(1,nch,sigc,0)
+    cat[...]=jnp.zeros_like(cat)
+    for s in range(cap):
+        cat[s,0:13,:]=jnp.concatenate([left[s].astype(F),right[s].astype(F)],1).astype(H)
+    trecv[ch]=tr[...]
+    def put(j,c):
+        h=lax.rem(me+j,nsec)
+        s=jnp.int32(0)
+        for k in range(NT):
+            g=slot_ref[0,h*NT+k]
+            s=s+jnp.where(g//cap==me,lax.rem(g,cap),0)
+        stage[j]=cat[s]
+        return c
+    lax.fori_loop(0,nsec,put,0)
+    pl.semaphore_wait(bar,nsec+nch-2)
+    def tcopy(j):
+        return pltpu.make_async_remote_copy(src_ref=tr,dst_ref=trecv.at[ch],send_sem=tssem.at[j],recv_sem=trsem.at[j],
+            device_id=(lax.rem(ch+j,nch),me),device_id_type=pl.DeviceIdType.MESH)
+    def ecopy(j):
+        return pltpu.make_async_remote_copy(src_ref=stage.at[j],dst_ref=recv.at[j],send_sem=ssem.at[j],recv_sem=rsem.at[j],
+            device_id=(ch,lax.rem(me+j,nsec)),device_id_type=pl.DeviceIdType.MESH)
+    lax.fori_loop(1,nch,lambda j,c:(tcopy(j).start(),c)[1],0)
+    lax.fori_loop(1,nsec,lambda j,c:(ecopy(j).start(),c)[1],0)
+    recv[0]=stage[0]
+    lax.fori_loop(1,nch,lambda j,c:(tcopy(j).wait(),c)[1],0)
+    trans_out[...]=trecv[...]
+    lax.fori_loop(1,nsec,lambda j,c:(ecopy(j).wait(),c)[1],0)
+    for t in range(NT):
+        o=slot_ref[0,me*NT+t]//cap
+        env_out[t]=recv[lax.rem(me-o+nsec,nsec)]
+
+def call_exchange(nsec,nch,left,right,slot,tr):
+    cap=left.shape[0]
+    return pl.pallas_call(functools.partial(exchange,nsec,nch),
+      out_shape=(jax.ShapeDtypeStruct((NT,16,1152),H),jax.ShapeDtypeStruct((nch,NT,576),F)),
+      in_specs=[pl.BlockSpec(memory_space=pltpu.VMEM)]*2+[pl.BlockSpec(memory_space=pltpu.SMEM),pl.BlockSpec(memory_space=pltpu.VMEM)],
+      out_specs=(pl.BlockSpec(memory_space=pltpu.VMEM),)*2,
+      scratch_shapes=[pltpu.VMEM((cap,16,1152),H),pltpu.VMEM((nsec,16,1152),H),pltpu.VMEM((nsec,16,1152),H),pltpu.VMEM((nch,NT,576),F),
+        pltpu.SemaphoreType.DMA((nsec,)),pltpu.SemaphoreType.DMA((nsec,)),pltpu.SemaphoreType.DMA((nch,)),pltpu.SemaphoreType.DMA((nch,))],
+      compiler_params=pltpu.CompilerParams(collective_id=0,has_side_effects=True,vmem_limit_bytes=16*2**20),
+      name="exchange")(left,right,slot,tr)
+
+def gather_solve(entries,nsec,kept_ref,st,v_ref,out_ref,en_ref,recv,ybuf,ssem,rsem):
+    me=lax.axis_index("sector"); ch=lax.axis_index("chain")
+    bar=pltpu.get_barrier_semaphore()
+    def sig(j,c):
+        pl.semaphore_signal(bar,inc=1,device_id=(ch,lax.rem(me+j,nsec)),device_id_type=pl.DeviceIdType.MESH)
+        return c
+    lax.fori_loop(1,nsec,sig,0)
+    recv[me]=st[...]
+    pl.semaphore_wait(bar,nsec-1)
+    def cp(j):
+        return pltpu.make_async_remote_copy(src_ref=st,dst_ref=recv.at[me],send_sem=ssem.at[j],recv_sem=rsem.at[j],
+            device_id=(ch,lax.rem(me+j,nsec)),device_id_type=pl.DeviceIdType.MESH)
+    lax.fori_loop(1,nsec,lambda j,c:(cp(j).start(),c)[1],0)
+    lax.fori_loop(1,nsec,lambda j,c:(cp(j).wait(),c)[1],0)
+    finish(entries,me,kept_ref,recv,v_ref,out_ref,en_ref,ybuf)
+
+def finish(entries,me,kept_ref,st_ref,v_ref,out_ref,en_ref,ybuf):
     lane=lax.broadcasted_iota(jnp.int32,(1,128),1)
-    z=jnp.zeros((96,128),F)
+    z=jnp.zeros((128-st_ref.shape[0],128),F)
     Q0=jnp.concatenate([st_ref[:,0,:],z],0).T
     Q1=jnp.concatenate([st_ref[:,1,:],z],0).T
     e,f=global_solve(lambda i:Q0[i:i+1,:],lambda i:Q1[i:i+1,:],entries)
@@ -237,34 +309,23 @@
         for t in range(NT):
             out_ref[t,:,24*p:24*p+24]=a[:,32*t:32*t+24]
 
-def call_k4(entries,me,kept,st,v):
-    return pl.pallas_call(functools.partial(k4,entries),
+def call_gather_solve(entries,nsec,kept,st,v):
+    return pl.pallas_call(functools.partial(gather_solve,entries,nsec),
       out_shape=(jax.ShapeDtypeStruct((4,24,384),F),jax.ShapeDtypeStruct((8,128),F)),
-      in_specs=[pl.BlockSpec(memory_space=pltpu.SMEM)]*2+[pl.BlockSpec(memory_space=pltpu.VMEM)]*2,
+      in_specs=[pl.BlockSpec(memory_space=pltpu.SMEM)]+[pl.BlockSpec(memory_space=pltpu.VMEM)]*2,
       out_specs=(pl.BlockSpec(memory_space=pltpu.VMEM),)*2,
-      scratch_shapes=[pltpu.VMEM((384,128),F)],
-      compiler_params=pltpu.CompilerParams(vmem_limit_bytes=16*2**20),
-      name="global_solve")(me,kept,st,v)
+      scratch_shapes=[pltpu.VMEM((nsec,8,128),F),pltpu.VMEM((384,128),F),pltpu.SemaphoreType.DMA((nsec,)),pltpu.SemaphoreType.DMA((nsec,))],
+      compiler_params=pltpu.CompilerParams(collective_id=1,has_side_effects=True,vmem_limit_bytes=16*2**20),
+      name="gather_solve")(kept,st,v)
 
 def body(wavefunction, transfer, left_env, right_env, pair_ops, env_slot, kept_ranks):
-    sector_count = lax.axis_size("sector")
-    me = lax.axis_index("sector")
+    nsec = lax.axis_size("sector")
+    nch = lax.axis_size("chain")
     chain = lax.axis_index("chain")
-    slots = left_env.shape[1]
-    trans = lax.all_gather(transfer[0], "chain")
-    slot_all = env_slot[0]
-    owner = slot_all // slots
-    within = slot_all - owner * slots
-    match = owner.reshape(sector_count, NT) == me
-    slot_of_home = jnp.sum(jnp.where(match, within.reshape(sector_count, NT), 0), axis=1)
-    env = jnp.concatenate([left_env[0], right_env[0]], axis=-1)
-    arrived = lax.all_to_all(env[slot_of_home], "sector", split_axis=0, concat_axis=0, tiled=True)
-    owner_mine = lax.dynamic_slice_in_dim(owner, me * NT, NT)
-    mine = arrived[owner_mine]
-    v, st = call_k2(chain.reshape(1), kept_ranks, trans, mine, wavefunction[0], pair_ops[0])
-    stats = lax.all_gather(st, "sector")
-    entries = float(sector_count * NT * NB * NP * NB)
-    out, en = call_k4(entries, me.reshape(1), kept_ranks, stats, v)
+    env, trans = call_exchange(nsec, nch, left_env[0], right_env[0], env_slot, transfer[0])
+    v, st = call_k2(chain.reshape(1), kept_ranks, trans, env, wavefunction[0], pair_ops[0])
+    entries = float(nsec * NT * NB * NP * NB)
+    out, en = call_gather_solve(entries, nsec, kept_ranks, st, v)
     return out[None], en[0, :1]
 
 

time: 112 us -> 74.6 us (0.67)
  blocking collectives: 54.5 us -> 0 us
  Pallas kernels: 19.6 us -> 70.3 us
  waiting for transfers between devices: 19.1 us -> 0 us
  starting transfers between devices: 11.6 us -> 0 us
  other arithmetic: 1.67 us -> 0 us
    all_gather x2 -> x0, blocking collectives: 54.5 us -> none  [the longest x1 43 us: body(): stats = lax.all_gather(st, 'sector')]
    pallas_call x1 -> x2, Pallas kernels: 3.34 us -> 54.1 us  [the longest x1 37.2 us: call_exchange(): pl.pallas_call(functools.partial(exchange, nsec, nch), out_shape=(jax.Sha...]
    all_to_all x1 -> x0, waiting for transfers between devices: 19.1 us -> none  [body(): lax.all_to_all(env[slot_of_home], 'sector', split_axis=0, concat_axis=0,...]
    all_to_all x1 -> x0, starting transfers between devices: 11.6 us -> none  [body(): lax.all_to_all(env[slot_of_home], 'sector', split_axis=0, concat_axis=0,...]
    gather x2 -> x0, local copies, waits for them, and re-layouts: 2.26 us -> none  [the longest x1 1.69 us: body(): env[slot_of_home]]
    unnamed x11, local copies, waits for them, and re-layouts: 0.53 us -> 1.94 us
    unnamed x1 -> x0, other arithmetic: 1.32 us -> none
  transfers between devices with their start and end apart: 1 -> 0, of which waited for: 1 -> 0; matrix products, arithmetic and copies ran while one was open for 0% -> 0% of each run, Pallas kernels for 0% -> 0%
where the time goes in v2:
time: 74.6 us; the launch traced here: 74.5 us
  Pallas kernels  70.3 us (94%)
  local copies, waits for them, and re-layouts  3.47 us (5%)
    pallas_call x1, Pallas kernels, call_exchange(): pl.pallas_call(functools.partial(exchange, nsec, nch), out_shape=(jax.Sha...  37.2 us
    pallas_call x1, Pallas kernels, call_gather_solve(): pl.pallas_call(functools.partial(gather_solve, entries, nsec), out_shape=...  16.9 us
    pallas_call x1, Pallas kernels, call_k2(): pl.pallas_call(k2, out_shape=(jax.ShapeDtypeStruct((5, 384, 128), F), jax...  16.2 us
    unnamed x11, local copies, waits for them, and re-layouts  1.94 us

profile of v2, /device:TPU:4, one launch (start us, length us, event | category | flops | bytes accessed | tf_op | source)
XLA Modules:
  0.0 74.5 jit_solution(4611696493317857054)
XLA Ops:
  0.6 0.0 copy-start.1
  0.6 1.0 %copy_bitcast_fusion = (bf16[8,13,576]{2,1,0:T(8,128)(2,1)S(1)}, bf16[8,13,576]{2,1,0:T(8,128)(2,1)S(1)}) fusion(bf16[1,8,13,576]{3,1,2,0:T(8,128)(2,1)} %param.10, bf16[1,8,13,576]{3,1,2,0:T(8,128)(2,1)} %param.9), kind=kLoop, calls=%fused_computation | loop fusion | bytes 479232 | tf_op jit(solution)/shard_map/squeeze | solution.py:325
  1.7 0.0 copy-start.4
  1.7 0.0 copy-done.1
  1.7 0.6 copy-done.4
  2.3 0.0 copy-start
  2.3 0.0 copy-start.2
  2.3 37.2 %exchange.1 = (bf16[4,16,1152]{2,1,0:T(8,128)(2,1)S(1)}, f32[8,4,576]{2,1,0:T(4,128)S(1)}) custom-call(bf16[8,13,576]{2,1,0:T(8,128)(2,1)S(1)} %get-tuple-element.15.left, bf16[8,13,576]{2,1,0:T(8,128)(2,1)S(1)} %get-tuple-element.14.right, s32[1,128]{1,0:T(1,128)S(1)} %copy-done.4, f32[4,576]{1,0:T(4,128)S(1)} %bitcast.12), custom_call_target="tpu_custom_call" | custom-call | tf_op jit(solution)/shard_map/exchange/pallas_call | solution.py:268
  39.5 0.0 copy-start.3
  39.5 0.0 copy-done
  39.5 0.0 copy-done.2
  39.5 0.6 copy-done.3
  40.1 16.2 %lanczos_local.1 = (f32[5,384,128]{2,1,0:T(8,128)S(1)}, f32[8,128]{1,0:T(8,128)S(1)}) custom-call(s32[1]{0:T(128)} %bitcast.chain_ref, s32[1,4]{1,0:T(1,128)S(1)} %copy-done.3, f32[8,4,576]{2,1,0:T(4,128)S(1)} %get-tuple-element.8.trans_ref, bf16[4,16,1152]{2,1,0:T(8,128)(2,1)S(1)} %get-tuple-element.9.env_ref, f32[4,24,384]{2,1,0:T(8,128)S(1)} %bitcast.10, ...), custom_call_target="tpu_custom_call" | custom-call | tf_op jit(solution)/shard_map/lanczos_local/pallas_call | solution.py:137
  56.4 16.9 %gather_solve.1 = (f32[4,24,384]{2,1,0:T(8,128)S(1)}, f32[8,128]{1,0:T(8,128)S(1)}) custom-call(s32[1,4]{1,0:T(1,128)S(1)} %copy-done.3, f32[8,128]{1,0:T(8,128)S(1)} %get-tuple-element.10.st, f32[5,384,128]{2,1,0:T(8,128)S(1)} %get-tuple-element.11.v_ref), custom_call_target="tpu_custom_call" | custom-call | tf_op jit(solution)/shard_map/gather_solve/pallas_call | solution.py:313
  73.3 0.5 slice.3
  73.8 0.7 copy.14
Async XLA Ops:
  0.6 1.0 %copy-start.1 = (f32[1,4,576]{2,1,0:T(4,128)S(1)}, f32[1,4,576]{2,1,0:T(4,128)}, u32[]{:S(2)}) copy-start(f32[1,4,576]{2,1,0:T(4,128)} %param.8) | copy-start | bytes 27652
  1.7 0.7 copy-start.4
  2.3 37.2 %copy-start = (f32[1,4,24,384]{3,2,1,0:T(8,128)S(1)}, f32[1,4,24,384]{3,2,1,0:T(8,128)}, u32[]{:S(2)}) copy-start(f32[1,4,24,384]{3,2,1,0:T(8,128)} %param.7) | copy-start | bytes 442372
  2.3 37.2 %copy-start.2 = (bf16[1,13,256]{2,1,0:T(8,128)(2,1)S(1)}, bf16[1,13,256]{2,1,0:T(8,128)(2,1)}, u32[]{:S(2)}) copy-start(bf16[1,13,256]{2,1,0:T(8,128)(2,1)} %param.11) | copy-start | bytes 19972
  39.5 0.7 copy-start.3

commit v3 on v1

v3 whole, which is shorter than its diff:
```python
import functools

import jax
import jax.numpy as jnp
from jax import lax
from jax.experimental import pallas as pl
from jax.experimental.pallas import tpu as pltpu
from jax.sharding import PartitionSpec as P

F = jnp.float32
H = jnp.bfloat16
NT = 4
NB = 24
NP = 16
NW = 13
MESH = pl.DeviceIdType.MESH


def split(x):
    h = x.astype(H)
    return h, (x - h.astype(F)).astype(H)


def grab(tile, off, t, lane):
    c0, o = off // 128, off % 128
    sh = (32 * t - o) % 128
    a = tile(c0)
    a = pltpu.roll(a, sh, 1) if sh else a
    if o + NB > 128:
        b = tile(c0 + 1)
        b = pltpu.roll(b, sh, 1) if sh else b
        a = jnp.where(lane < 32 * t + 128 - o, a, b)
    return jnp.where((lane >= 32 * t) & (lane < 32 * t + NB), a, 0.0)


def full(x):
    return jnp.sum(jnp.sum(x, axis=0, keepdims=True), axis=1, keepdims=True)


def inverse(n):
    return jnp.where(n > 0, 1.0 / n, 0.0)


def loop(a, b, f):
    def step(j, c):
        f(j)
        return c

    lax.fori_loop(a, b, step, 0)


def global_solve(q0,q1,entries):
    tot=lambda x: jnp.sum(x,axis=1,keepdims=True)
    pos={}
    n=0
    for i in range(4):
        for j in range(i,5):
            pos[i,j]=n; n+=1
    M=[[q0(pos[min(i,j),max(i,j)]) for j in range(4)] for i in range(4)]
    Mk=[[q1(pos[min(i,j),max(i,j)]) for j in range(4)] for i in range(4)]
    Wv=[q0(pos[i,4]) for i in range(4)]
    n0=q0(16); al=[q0(17+i) for i in range(3)]; be=[q0(20+i) for i in range(3)]
    def tmul(c):
        k=len(c)-1
        y=[None]*min(k+2,4)
        def add(i,z):
            y[i]=z if y[i] is None else y[i]+z
        for j in range(min(k+1,3)):
            add(j,al[j]*c[j]); add(j+1,be[j]*c[j])
            if j>0: add(j-1,be[j-1]*c[j])
        return y
    def dot(Mx,a,b):
        acc=None
        for i in range(len(a)):
            s=None
            for j in range(len(b)):
                z=Mx[i][j]*b[j]; s=z if s is None else s+z
            s=s*a[i]; acc=s if acc is None else acc+s
        return acc
    c=[n0/jnp.sqrt(tot(n0*n0))]
    cp=[]; b=None
    cs=[]; A=[]; Bt=[]
    for k in range(4):
        cs.append(c)
        y=tmul(c)
        g=dot(M,c,y)
        if k==3:
            s=None
            for i in range(4):
                z=c[i]*Wv[i]; s=z if s is None else s+z
            g=g+s*c[3]
        a=tot(g); A.append(a)
        if k<3:
            r=[]
            for i in range(len(y)):
                z=y[i]
                if i<len(c): z=z-a*c[i]
                if i<len(cp): z=z-b*cp[i]
                r.append(z)
            b=jnp.sqrt(tot(dot(M,r,r))); Bt.append(b)
            cp=c; c=[z/b for z in r]
    ab=[jnp.abs(z) for z in Bt]
    bounds=[A[0]-ab[0],A[1]-ab[0]-ab[1],A[2]-ab[1]-ab[2],A[3]-ab[2]]
    init=jnp.minimum(jnp.minimum(bounds[0],bounds[1]),jnp.minimum(bounds[2],bounds[3]))-1.0
    B2=[z*z for z in Bt]
    def newton(_,e):
        vp=jnp.ones_like(e); vn=A[0]-e; sp=jnp.zeros_like(e); sn=-jnp.ones_like(e)
        for p in range(1,4):
            sh=A[p]-e; w=B2[p-1]
            v2=sh*vn-w*vp; s2=sh*sn-vn-w*sp
            vp,vn=vn,v2; sp,sn=sn,s2
        return e-vn/sn
    e=lax.fori_loop(0,40,newton,init)
    co=[jnp.ones_like(e),(e-A[0])/Bt[0]]
    for p in range(1,3):
        co.append(((e-A[p])*co[p]-Bt[p-1]*co[p-1])/Bt[p])
    nrm=jnp.sqrt(co[0]*co[0]+co[1]*co[1]+co[2]*co[2]+co[3]*co[3])
    f=[None]*4
    for k in range(4):
        for i in range(len(cs[k])):
            z=(co[k]/nrm)*cs[k][i]; f[i]=z if f[i] is None else f[i]+z
    scale=jnp.sqrt(entries/tot(dot(Mk,f,f)))
    return e,[z*scale for z in f]


def whole(
    entries, nsec, nch,
    left, right, slot_ref, tr, x_ref, b_ref, kept_ref,
    out_ref, en_ref,
    wide, wire, cat, stage, recv0, recv1, trecv, v_ref, st, strecv,
    tpad, tbd, ebd, b2, c2, mixed, moved, acat, ybuf,
    ssem, rsem, tssem, trsem, qssem, qrsem,
):
    me = lax.axis_index("sector")
    ch = lax.axis_index("chain")
    cap = left.shape[1]
    lane = lax.broadcasted_iota(jnp.int32, (1, 128), 1)
    tl = lane // 32
    bar = pltpu.get_barrier_semaphore()
    loop(1, nsec, lambda j: pl.semaphore_signal(bar, inc=1, device_id=(ch, lax.rem(me + j, nsec)), device_id_type=MESH))
    loop(1, nch, lambda j: pl.semaphore_signal(bar, inc=1, device_id=(lax.rem(ch + j, nch), me), device_id_type=MESH))
    wire[...] = jnp.zeros_like(wire)
    for side, src in ((0, right), (1, left)):
        for w in range(NW):
            row8 = src[w].astype(F)
            for c in range(4):
                wide[c, cap * w:cap * w + cap, :] = row8[:, 128 * c:128 * c + 128]
            wide[4, cap * w:cap * w + cap, 0:64] = row8[:, 512:576]
        for s in range(cap):
            for c in range(4):
                wire[s, 13 * c:13 * c + 13, :] = wide[c, pl.ds(s, 13, stride=cap), :]
            lo = wide[4, pl.ds(s, 7, stride=cap), :]
            hi = pltpu.roll(wide[4, pl.ds(s + 7 * cap, 6, stride=cap), :], 64, 1)
            wire[s, 52:59, :] = jnp.where(lane < 64, lo, 0.0)
            wire[s, 52:58, :] = jnp.where(lane < 64, lo[0:6], hi)
        cat[side] = wire[...].astype(H)
    trecv[ch] = tr[...]

    def put(j):
        h = lax.rem(me + j, nsec)
        s = jnp.int32(0)
        for k in range(NT):
            g = slot_ref[0, h * NT + k]
            s = s + jnp.where(g // cap == me, lax.rem(g, cap), 0)
        stage[0, j] = cat[0, s]
        stage[1, j] = cat[1, s]

    loop(0, nsec, put)
    pl.semaphore_wait(bar, nsec + nch - 2)

    def tcopy(j):
        return pltpu.make_async_remote_copy(
            src_ref=tr, dst_ref=trecv.at[ch], send_sem=tssem.at[j], recv_sem=trsem.at[j],
            device_id=(lax.rem(ch + j, nch), me), device_id_type=MESH)

    def ecopy(side, j):
        return pltpu.make_async_remote_copy(
            src_ref=stage.at[side, j], dst_ref=(recv0, recv1)[side].at[j], send_sem=ssem.at[side, j], recv_sem=rsem.at[side, j],
            device_id=(ch, lax.rem(me + j, nsec)), device_id_type=MESH)

    loop(1, nch, lambda j: tcopy(j).start())
    loop(1, nsec, lambda j: ecopy(0, j).start())
    loop(1, nsec, lambda j: ecopy(1, j).start())
    recv0[0] = stage[0, 0]
    recv1[0] = stage[1, 0]

    bf = b_ref[...].astype(F)
    for q in range(NP):
        off = 16 * q
        a = bf[:, (off // 128) * 128:(off // 128) * 128 + 128]
        sh = (-(off % 128)) % 128
        a = pltpu.roll(a, sh, 1) if sh else a
        tbd[pl.ds(q, NW, stride=NP), :] = jnp.where(lane < 16, a, 0.0)
    bb = tbd[0:208, :]
    b2[...] = (bb + pltpu.roll(bb, 16, 1))[:, :32].astype(H)
    for p in range(NP):
        acc = jnp.zeros((NB, 128), F)
        for t in range(NT):
            acc = acc + grab(lambda c: x_ref[t, :, c * 128:(c + 1) * 128], NB * p, t, lane)
        v_ref[0, pl.ds(p, NB, stride=NP), :] = acc
    x = v_ref[0]
    n0 = jnp.sqrt(full(x * x))
    v_ref[0] = x * inverse(n0)
    loop(1, nch, lambda j: tcopy(j).wait())
    tbd[...] = jnp.zeros_like(tbd)
    for t in range(NT):
        tpad[0:8, 0:576] = trecv[:, t, :]
        for i in range(NB):
            tbd[pl.ds(32 * t + i, 8, stride=128), :] = grab(lambda c: tpad[0:8, c * 128:(c + 1) * 128], NB * i, t, lane)
    row = lax.broadcasted_iota(jnp.int32, (128, 128), 0)
    col = lax.broadcasted_iota(jnp.int32, (128, 128), 1)
    eye = (row == col).astype(F)
    T = [jnp.where(ch > c, tbd[c * 128:(c + 1) * 128, :], eye) for c in range(7)]

    def mm(a, b):
        return jnp.dot(a, b, precision=lax.Precision.HIGHEST, preferred_element_type=F)

    pre = mm(mm(T[6], mm(T[5], T[4])), mm(mm(T[3], T[2]), mm(T[1], T[0])))
    ph, plo = split(pre.T)

    ebd[...] = jnp.zeros_like(ebd)

    def spread(side):
        for t in range(NT):
            o = slot_ref[0, me * NT + t] // cap
            wire[t] = (recv0, recv1)[side][lax.rem(me - o + nsec, nsec)].astype(F)
            tpad[0:7, 0:128] = wire[t, 52:59, :]
            tpad[7:13, 0:128] = pltpu.roll(wire[t, 52:58, :], 64, 1)
            tile = lambda c: wire[t, 13 * c:13 * c + 13, :] if c < 4 else tpad[0:13, 0:128]
            for i in range(NB):
                ebd[pl.ds(32 * t + i, NW, stride=128), :] = grab(tile, NB * i, t, lane)

    def pair_step(k):
        bm = b2[...]
        for l in range(0, NB, 2):
            xx = jnp.concatenate([v_ref[k, 16 * l:16 * l + 16, :], v_ref[k, 16 * l + 16:16 * l + 32, :]], 1)
            h, lo = split(xx)
            o = jnp.dot(bm, jnp.concatenate([h, lo], 0), preferred_element_type=F)
            h, lo = split(o)
            mixed[0, l] = h[:, :128]
            mixed[0, l + 1] = h[:, 128:]
            mixed[1, l] = lo[:, :128]
            mixed[1, l + 1] = lo[:, 128:]

    def right_step():
        for w in range(NW):
            h = mixed[0, :, 16 * w:16 * w + 16, :].reshape(384, 128)
            lo = mixed[1, :, 16 * w:16 * w + 16, :].reshape(384, 128)
            moved[w] = jnp.dot(jnp.concatenate([h, lo], 1), c2[w], preferred_element_type=F)

    def left_step(k, a2):
        for q in range(0, NP, 2):
            r = jnp.concatenate([jnp.concatenate([moved[w, pl.ds(q + j, NB, stride=NP), :] for w in range(NW)], 0) for j in range(2)], 1)
            h = r.astype(H).astype(F)
            o = jnp.dot(a2, jnp.concatenate([h, r - h], 0).astype(H), preferred_element_type=F)
            for j in range(2):
                oj = o[:, 128 * j:128 * j + 128]
                y = jnp.where(tl == 0, oj[0:24], jnp.where(tl == 1, oj[24:48], jnp.where(tl == 2, oj[48:72], oj[72:96])))
                v_ref[k + 1, pl.ds(q + j, NB, stride=NP), :] = y

    pair_step(0)
    loop(1, nsec, lambda j: ecopy(0, j).wait())
    spread(0)
    for w in range(NW):
        ct = ebd[w * 128:(w + 1) * 128, :].T.astype(H)
        c2[w, 0:128, :] = ct
        c2[w, 128:256, :] = ct
    right_step()
    loop(1, nsec, lambda j: ecopy(1, j).wait())
    spread(1)
    pp = jnp.concatenate([ph, plo], 0)
    pq = jnp.concatenate([ph, plo, ph], 0)
    for w in range(NW):
        e = ebd[w * 128:(w + 1) * 128, :].astype(H)
        s = jnp.dot(jnp.concatenate([e, e], 1), pp, preferred_element_type=F)
        sh, sl = split(s.T)
        at = jnp.dot(jnp.concatenate([sh, sh, sl], 1), pq, preferred_element_type=F)
        acat[24 * w:24 * w + 24, :] = at[0:24] + at[32:56] + at[64:88] + at[96:120]
    acat[312:384, :] = jnp.zeros((72, 128), F)
    al = acat[...].T
    al = jnp.concatenate([al[32 * t:32 * t + 24] for t in range(NT)], 0)[:, :312].astype(H).astype(F)
    a2 = jnp.concatenate([al, al], 1).astype(H)

    alphas = []
    betas = []
    for k in range(4):
        if k > 0:
            pair_step(k)
            right_step()
        left_step(k, a2)
        if k < 3:
            y = v_ref[k + 1]
            a = full(v_ref[k] * y)
            r = y - a * v_ref[k]
            if k > 0:
                r = r - betas[-1] * v_ref[k - 1]
            b = jnp.sqrt(full(r * r))
            alphas.append(a)
            betas.append(b)
            v_ref[k + 1] = r * inverse(b)
    rows = []
    for i in range(4):
        for j in range(i, 5):
            rows.append(jnp.sum(v_ref[i] * v_ref[j], axis=0, keepdims=True))
    g = jnp.concatenate(rows + [jnp.zeros((114, 128), F)], 0)
    kp = jnp.where(tl == 0, kept_ref[0, 0], jnp.where(tl == 1, kept_ref[0, 1], jnp.where(tl == 2, kept_ref[0, 2], kept_ref[0, 3])))
    keep = lax.rem(lane, 32) < kp
    r8 = lax.broadcasted_iota(jnp.int32, (8, 128), 0)
    lhs = jnp.where(r8 == 0, 1.0, jnp.where((r8 == 1) & keep, 1.0, 0.0))
    s = lax.dot_general(lhs, g, (((1,), (1,)), ((), ())), precision=lax.Precision.HIGHEST, preferred_element_type=F)
    for i, val in enumerate([n0] + alphas + betas):
        s = s + jnp.where((lane == 16 + i) & (r8 == 0), val, 0.0)
    st[...] = s

    def qcopy(j):
        return pltpu.make_async_remote_copy(
            src_ref=st, dst_ref=strecv.at[me], send_sem=qssem.at[j], recv_sem=qrsem.at[j],
            device_id=(ch, lax.rem(me + j, nsec)), device_id_type=MESH)

    loop(1, nsec, lambda j: qcopy(j).start())
    strecv[me] = s
    loop(1, nsec, lambda j: qcopy(j).wait())
    z = jnp.zeros((128 - nsec, 128), F)
    q0 = jnp.concatenate([strecv[:, 0, :], z], 0).T
    q1 = jnp.concatenate([strecv[:, 1, :], z], 0).T
    e, f = global_solve(lambda i: q0[i:i + 1, :], lambda i: q1[i:i + 1, :], entries)
    en_ref[...] = jnp.broadcast_to(e, (8, 128))
    mine = [jnp.sum(jnp.where(lane == me, c, 0.0), axis=1, keepdims=True) for c in f]
    y = mine[0] * v_ref[0]
    for i in range(1, 4):
        y = y + mine[i] * v_ref[i]
    ybuf[...] = jnp.where(keep, y, 0.0)
    for p in range(NP):
        a = ybuf[pl.ds(p, NB, stride=NP), :]
        for t in range(NT):
            out_ref[t, :, NB * p:NB * p + NB] = a[:, 32 * t:32 * t + NB]


def body(wavefunction, transfer, left_env, right_env, pair_ops, env_slot, kept_ranks):
    nsec = lax.axis_size("sector")
    nch = lax.axis_size("chain")
    cap = left_env.shape[1]
    entries = float(nsec * NT * NB * NP * NB)
    vmem = pl.BlockSpec(memory_space=pltpu.VMEM)
    smem = pl.BlockSpec(memory_space=pltpu.SMEM)
    dma = pltpu.SemaphoreType.DMA
    out, en = pl.pallas_call(
        functools.partial(whole, entries, nsec, nch),
        out_shape=(jax.ShapeDtypeStruct((NT, NB, NP * NB), F), jax.ShapeDtypeStruct((8, 128), F)),
        in_specs=[vmem, vmem, smem, vmem, vmem, vmem, smem],
        out_specs=(vmem, vmem),
        scratch_shapes=[
            pltpu.VMEM((5, cap * NW, 128), F),
            pltpu.VMEM((cap, 64, 128), F),
            pltpu.VMEM((2, cap, 64, 128), H),
            pltpu.VMEM((2, nsec, 64, 128), H),
            pltpu.VMEM((nsec, 64, 128), H),
            pltpu.VMEM((nsec, 64, 128), H),
            pltpu.VMEM((nch, NT, 576), F),
            pltpu.VMEM((5, 384, 128), F),
            pltpu.VMEM((8, 128), F),
            pltpu.VMEM((nsec, 8, 128), F),
            pltpu.VMEM((16, 640), F),
            pltpu.VMEM((1024, 128), F),
            pltpu.VMEM((1664, 128), F),
            pltpu.VMEM((208, 32), H),
            pltpu.VMEM((NW, 256, 128), H),
            pltpu.VMEM((2, NB, 208, 128), H),
            pltpu.VMEM((NW, 384, 128), F),
            pltpu.VMEM((384, 128), F),
            pltpu.VMEM((384, 128), F),
            dma((2, nsec)), dma((2, nsec)), dma((nch,)), dma((nch,)), dma((nsec,)), dma((nsec,)),
        ],
        compiler_params=pltpu.CompilerParams(collective_id=0, has_side_effects=True, vmem_limit_bytes=40 * 2**20),
        name="lanczos",
    )(
        jnp.swapaxes(left_env[0], 0, 1), jnp.swapaxes(right_env[0], 0, 1), env_slot, transfer[0], wavefunction[0],
        pair_ops[0], kept_ranks,
    )
    return out[None], en[0, :1]


def solution(mesh):
    return jax.shard_map(
        body,
        mesh=mesh,
        in_specs=(
            P("chain", "sector", None, None),
            P("chain", "sector", None),
            P("chain", "sector", None, None),
            P("chain", "sector", None, None),
            P("chain", None, None),
            P("chain", None),
            P("chain", "sector"),
        ),
        out_specs=(P("chain", "sector", None, None), P("chain")),
        check_vma=False,
    )
```

time: 112 us -> 67.1 us (0.60)
  blocking collectives: 54.5 us -> 0 us
  Pallas kernels: 19.6 us -> 60.9 us
  waiting for transfers between devices: 19.1 us -> 0 us
  starting transfers between devices: 11.6 us -> 0 us
  other arithmetic: 1.67 us -> 0 us
    all_gather x2 -> x0, blocking collectives: 54.5 us -> none  [the longest x1 43 us: body(): stats = lax.all_gather(st, 'sector')]
    pallas_call x2 -> x1, Pallas kernels: 19.6 us -> 60.9 us  [body(): pl.pallas_call(functools.partial(whole, entries, nsec, nch), out_shape=(j...]
    all_to_all x1 -> x0, waiting for transfers between devices: 19.1 us -> none  [body(): lax.all_to_all(env[slot_of_home], 'sector', split_axis=0, concat_axis=0,...]
    all_to_all x1 -> x0, starting transfers between devices: 11.6 us -> none  [body(): lax.all_to_all(env[slot_of_home], 'sector', split_axis=0, concat_axis=0,...]
    unnamed x11 -> x15, local copies, waits for them, and re-layouts: 0.53 us -> 4.76 us
    gather x2 -> x0, local copies, waits for them, and re-layouts: 2.26 us -> none  [the longest x1 1.69 us: body(): env[slot_of_home]]
    unnamed x1 -> x0, other arithmetic: 1.32 us -> none
  transfers between devices with their start and end apart: 1 -> 0, of which waited for: 1 -> 0; matrix products, arithmetic and copies ran while one was open for 0% -> 0% of each run, Pallas kernels for 0% -> 0%
where the time goes in v3:
time: 67.1 us; the launch traced here: 66.9 us
  Pallas kernels  60.9 us (91%)
  local copies, waits for them, and re-layouts  5.27 us (8%)
    pallas_call x1, Pallas kernels, body(): pl.pallas_call(functools.partial(whole, entries, nsec, nch), out_shape=(j...  60.9 us
    unnamed x15, local copies, waits for them, and re-layouts  4.76 us

profile of v3, /device:TPU:4, one launch (start us, length us, event | category | flops | bytes accessed | tf_op | source)
XLA Modules:
  0.0 66.9 jit_solution(1059291704407080282)
XLA Ops:
  0.6 0.0 copy-start.4
  0.6 0.0 copy-start.5
  0.7 0.0 copy-start.6
  0.7 0.7 copy-done.4
  1.3 0.0 copy-done.5
  1.3 0.0 copy-done.6
  1.3 0.0 copy-start
  1.3 0.9 %copy-done = f32[1,4,24,384]{3,2,1,0:T(8,128)S(1)} copy-done((f32[1,4,24,384]{3,2,1,0:T(8,128)S(1)}, f32[1,4,24,384]{3,2,1,0:T(8,128)}, u32[]{:S(2)}) %copy-start) | copy-done | bytes 147480
  2.2 0.0 copy-start.1
  2.2 0.9 %copy-done.1 = bf16[1,8,13,576]{3,1,2,0:T(8,128)(2,1)S(1)} copy-done((bf16[1,8,13,576]{3,1,2,0:T(8,128)(2,1)S(1)}, bf16[1,8,13,576]{3,1,2,0:T(8,128)(2,1)}, u32[]{:S(2)}) %copy-start.1) | copy-done | bytes 119832
  3.2 0.0 copy-start.2
  3.2 0.9 %copy-done.2 = bf16[1,8,13,576]{3,1,2,0:T(8,128)(2,1)S(1)} copy-done((bf16[1,8,13,576]{3,1,2,0:T(8,128)(2,1)S(1)}, bf16[1,8,13,576]{3,1,2,0:T(8,128)(2,1)}, u32[]{:S(2)}) %copy-start.2) | copy-done | bytes 119832
  4.1 0.0 copy-start.3
  4.1 0.7 %copy-done.3 = f32[1,4,576]{2,1,0:T(4,128)S(1)} copy-done((f32[1,4,576]{2,1,0:T(4,128)S(1)}, f32[1,4,576]{2,1,0:T(4,128)}, u32[]{:S(2)}) %copy-start.3) | copy-done | bytes 9240
  4.8 60.9 %lanczos.1 = (f32[4,24,384]{2,1,0:T(8,128)S(1)}, f32[8,128]{1,0:T(8,128)S(1)}) custom-call(bf16[13,8,576]{2,1,0:T(8,128)(2,1)S(1)} %bitcast.13, bf16[13,8,576]{2,1,0:T(8,128)(2,1)S(1)} %bitcast.14, s32[1,128]{1,0:T(1,128)S(1)} %copy-done.5, f32[4,576]{1,0:T(4,128)S(1)} %bitcast.15, f32[4,24,384]{2,1,0:T(8,128)S(1)} %bitcast.11, ...), custom_call_target="tpu_custom_call" | custom-call | tf_op jit(solution)/shard_map/lanczos/pallas_call | solution.py:347
  65.7 0.5 slice.3
  66.2 0.7 copy.10
Async XLA Ops:
  0.6 0.7 %copy-start.4 = (bf16[1,13,256]{2,1,0:T(8,128)(2,1)S(1)}, bf16[1,13,256]{2,1,0:T(8,128)(2,1)}, u32[]{:S(2)}) copy-start(bf16[1,13,256]{2,1,0:T(8,128)(2,1)} %param.11) | copy-start | bytes 19972
  0.6 0.7 %copy-start.5 = (s32[1,128]{1,0:T(1,128)S(1)}, s32[1,128]{1,0:T(1,128)}, u32[]{:S(2)}) copy-start(s32[1,128]{1,0:T(1,128)} %slot_ref.1) | copy-start | bytes 1540
  0.7 0.7 %copy-start.6 = (s32[1,4]{1,0:T(1,128)S(1)}, s32[1,4]{1,0:T(1,128)}, u32[]{:S(2)}) copy-start(s32[1,4]{1,0:T(1,128)} %kept_ref.1) | copy-start | bytes 52
  1.3 0.9 %copy-start = (f32[1,4,24,384]{3,2,1,0:T(8,128)S(1)}, f32[1,4,24,384]{3,2,1,0:T(8,128)}, u32[]{:S(2)}) copy-start(f32[1,4,24,384]{3,2,1,0:T(8,128)} %param.7) | copy-start | bytes 442372
  2.2 0.9 %copy-start.1 = (bf16[1,8,13,576]{3,1,2,0:T(8,128)(2,1)S(1)}, bf16[1,8,13,576]{3,1,2,0:T(8,128)(2,1)}, u32[]{:S(2)}) copy-start(bf16[1,8,13,576]{3,1,2,0:T(8,128)(2,1)} %param.9) | copy-start | bytes 359428
  3.2 0.9 %copy-start.2 = (bf16[1,8,13,576]{3,1,2,0:T(8,128)(2,1)S(1)}, bf16[1,8,13,576]{3,1,2,0:T(8,128)(2,1)}, u32[]{:S(2)}) copy-start(bf16[1,8,13,576]{3,1,2,0:T(8,128)(2,1)} %param.10) | copy-start | bytes 359428
  4.1 0.7 %copy-start.3 = (f32[1,4,576]{2,1,0:T(4,128)S(1)}, f32[1,4,576]{2,1,0:T(4,128)}, u32[]{:S(2)}) copy-start(f32[1,4,576]{2,1,0:T(4,128)} %param.8) | copy-start | bytes 27652

commit v4 on v3

--- a/solution.py
+++ b/solution.py
@@ -125,22 +125,30 @@
 
 def whole(
     entries, nsec, nch,
-    left, right, slot_ref, tr, x_ref, b_ref, kept_ref,
+    left_in, right_in, slot_in, tr_in, x_in, b_in, kept_in,
     out_ref, en_ref,
+    left, right, slot_ref, tr, x_ref, b_ref, kept_ref, lsem,
     wide, wire, cat, stage, recv0, recv1, trecv, v_ref, st, strecv,
     tpad, tbd, ebd, b2, c2, mixed, moved, acat, ybuf,
     ssem, rsem, tssem, trsem, qssem, qrsem,
 ):
     me = lax.axis_index("sector")
     ch = lax.axis_index("chain")
-    cap = left.shape[1]
+    cap = left_in.shape[1]
     lane = lax.broadcasted_iota(jnp.int32, (1, 128), 1)
     tl = lane // 32
+    loads = [
+        pltpu.make_async_copy(a, b, lsem.at[i])
+        for i, (a, b) in enumerate((
+            (slot_in, slot_ref), (left_in, left), (tr_in, tr), (right_in, right), (b_in, b_ref), (x_in, x_ref), (kept_in, kept_ref)))
+    ]
+    for c in loads:
+        c.start()
     bar = pltpu.get_barrier_semaphore()
     loop(1, nsec, lambda j: pl.semaphore_signal(bar, inc=1, device_id=(ch, lax.rem(me + j, nsec)), device_id_type=MESH))
     loop(1, nch, lambda j: pl.semaphore_signal(bar, inc=1, device_id=(lax.rem(ch + j, nch), me), device_id_type=MESH))
-    wire[...] = jnp.zeros_like(wire)
-    for side, src in ((0, right), (1, left)):
+    def pack(side, src, chosen):
+        wire[...] = jnp.zeros_like(wire)
         for w in range(NW):
             row8 = src[w].astype(F)
             for c in range(4):
@@ -154,35 +162,43 @@
             wire[s, 52:59, :] = jnp.where(lane < 64, lo, 0.0)
             wire[s, 52:58, :] = jnp.where(lane < 64, lo[0:6], hi)
         cat[side] = wire[...].astype(H)
-    trecv[ch] = tr[...]
-
-    def put(j):
+        for j in range(nsec):
+            stage[side, j] = cat[side, chosen[j]]
+
+    def tcopy(j):
+        return pltpu.make_async_remote_copy(
+            src_ref=tr, dst_ref=trecv.at[ch], send_sem=tssem.at[j], recv_sem=trsem.at[j],
+            device_id=(lax.rem(ch + j, nch), me), device_id_type=MESH)
+
+    def ecopy(side, j):
+        return pltpu.make_async_remote_copy(
+            src_ref=stage.at[side, j], dst_ref=(recv0, recv1)[side].at[j], send_sem=ssem.at[side, j], recv_sem=rsem.at[side, j],
+            device_id=(ch, lax.rem(me + j, nsec)), device_id_type=MESH)
+
+    loads[0].wait()
+    chosen = []
+    for j in range(nsec):
         h = lax.rem(me + j, nsec)
         s = jnp.int32(0)
         for k in range(NT):
             g = slot_ref[0, h * NT + k]
             s = s + jnp.where(g // cap == me, lax.rem(g, cap), 0)
-        stage[0, j] = cat[0, s]
-        stage[1, j] = cat[1, s]
-
-    loop(0, nsec, put)
+        chosen.append(s)
+    loads[1].wait()
+    pack(1, left, chosen)
+    loads[2].wait()
+    trecv[ch] = tr[...]
     pl.semaphore_wait(bar, nsec + nch - 2)
-
-    def tcopy(j):
-        return pltpu.make_async_remote_copy(
-            src_ref=tr, dst_ref=trecv.at[ch], send_sem=tssem.at[j], recv_sem=trsem.at[j],
-            device_id=(lax.rem(ch + j, nch), me), device_id_type=MESH)
-
-    def ecopy(side, j):
-        return pltpu.make_async_remote_copy(
-            src_ref=stage.at[side, j], dst_ref=(recv0, recv1)[side].at[j], send_sem=ssem.at[side, j], recv_sem=rsem.at[side, j],
-            device_id=(ch, lax.rem(me + j, nsec)), device_id_type=MESH)
-
     loop(1, nch, lambda j: tcopy(j).start())
+    loop(1, nsec, lambda j: ecopy(1, j).start())
+    loads[3].wait()
+    pack(0, right, chosen)
     loop(1, nsec, lambda j: ecopy(0, j).start())
-    loop(1, nsec, lambda j: ecopy(1, j).start())
     recv0[0] = stage[0, 0]
     recv1[0] = stage[1, 0]
+    loads[4].wait()
+    loads[5].wait()
+    loads[6].wait()
 
     bf = b_ref[...].astype(F)
     for q in range(NP):
@@ -259,13 +275,6 @@
                 v_ref[k + 1, pl.ds(q + j, NB, stride=NP), :] = y
 
     pair_step(0)
-    loop(1, nsec, lambda j: ecopy(0, j).wait())
-    spread(0)
-    for w in range(NW):
-        ct = ebd[w * 128:(w + 1) * 128, :].T.astype(H)
-        c2[w, 0:128, :] = ct
-        c2[w, 128:256, :] = ct
-    right_step()
     loop(1, nsec, lambda j: ecopy(1, j).wait())
     spread(1)
     pp = jnp.concatenate([ph, plo], 0)
@@ -280,6 +289,13 @@
     al = acat[...].T
     al = jnp.concatenate([al[32 * t:32 * t + 24] for t in range(NT)], 0)[:, :312].astype(H).astype(F)
     a2 = jnp.concatenate([al, al], 1).astype(H)
+    loop(1, nsec, lambda j: ecopy(0, j).wait())
+    spread(0)
+    for w in range(NW):
+        ct = ebd[w * 128:(w + 1) * 128, :].T.astype(H)
+        c2[w, 0:128, :] = ct
+        c2[w, 128:256, :] = ct
+    right_step()
 
     alphas = []
     betas = []
@@ -324,7 +340,7 @@
     q0 = jnp.concatenate([strecv[:, 0, :], z], 0).T
     q1 = jnp.concatenate([strecv[:, 1, :], z], 0).T
     e, f = global_solve(lambda i: q0[i:i + 1, :], lambda i: q1[i:i + 1, :], entries)
-    en_ref[...] = jnp.broadcast_to(e, (8, 128))
+    en_ref[...] = e
     mine = [jnp.sum(jnp.where(lane == me, c, 0.0), axis=1, keepdims=True) for c in f]
     y = mine[0] * v_ref[0]
     for i in range(1, 4):
@@ -342,14 +358,22 @@
     cap = left_env.shape[1]
     entries = float(nsec * NT * NB * NP * NB)
     vmem = pl.BlockSpec(memory_space=pltpu.VMEM)
-    smem = pl.BlockSpec(memory_space=pltpu.SMEM)
+    hbm = pl.BlockSpec(memory_space=pltpu.HBM)
     dma = pltpu.SemaphoreType.DMA
     out, en = pl.pallas_call(
         functools.partial(whole, entries, nsec, nch),
-        out_shape=(jax.ShapeDtypeStruct((NT, NB, NP * NB), F), jax.ShapeDtypeStruct((8, 128), F)),
-        in_specs=[vmem, vmem, smem, vmem, vmem, vmem, smem],
+        out_shape=(jax.ShapeDtypeStruct((NT, NB, NP * NB), F), jax.ShapeDtypeStruct((1, 1), F)),
+        in_specs=[hbm] * 7,
         out_specs=(vmem, vmem),
         scratch_shapes=[
+            pltpu.VMEM((NW, cap, 576), H),
+            pltpu.VMEM((NW, cap, 576), H),
+            pltpu.SMEM(env_slot.shape, jnp.int32),
+            pltpu.VMEM(transfer.shape[1:], F),
+            pltpu.VMEM(wavefunction.shape[1:], F),
+            pltpu.VMEM(pair_ops.shape[1:], H),
+            pltpu.SMEM(kept_ranks.shape, jnp.int32),
+            dma((7,)),
             pltpu.VMEM((5, cap * NW, 128), F),
             pltpu.VMEM((cap, 64, 128), F),
             pltpu.VMEM((2, cap, 64, 128), H),
@@ -371,13 +395,13 @@
             pltpu.VMEM((384, 128), F),
             dma((2, nsec)), dma((2, nsec)), dma((nch,)), dma((nch,)), dma((nsec,)), dma((nsec,)),
         ],
-        compiler_params=pltpu.CompilerParams(collective_id=0, has_side_effects=True, vmem_limit_bytes=40 * 2**20),
+        compiler_params=pltpu.CompilerParams(collective_id=0, has_side_effects=True, vmem_limit_bytes=64 * 2**20),
         name="lanczos",
     )(
         jnp.swapaxes(left_env[0], 0, 1), jnp.swapaxes(right_env[0], 0, 1), env_slot, transfer[0], wavefunction[0],
         pair_ops[0], kept_ranks,
     )
-    return out[None], en[0, :1]
+    return out[None], en.reshape(1)
 
 
 def solution(mesh):

time: 67.1 us -> 63.2 us (0.942)
  local copies, waits for them, and re-layouts: 5.27 us -> 1.58 us
  Pallas kernels: 60.9 us -> 59.1 us
  between operations: 0.67 us -> 2.4 us
    unnamed x15 -> x1, local copies, waits for them, and re-layouts: 4.76 us -> 1.58 us
    pallas_call x1, Pallas kernels: 60.9 us -> 59.1 us  [body(): pl.pallas_call(functools.partial(whole, entries, nsec, nch), out_shape=(j...]
where the time goes in v4:
time: 63.2 us; the launch traced here: 63.1 us
  Pallas kernels  59.1 us (94%)
  between operations  2.4 us (4%)
  local copies, waits for them, and re-layouts  1.58 us (2%)
    pallas_call x1, Pallas kernels, body(): pl.pallas_call(functools.partial(whole, entries, nsec, nch), out_shape=(j...  59.1 us
    unnamed x1, local copies, waits for them, and re-layouts  1.58 us

profile of v4, /device:TPU:4, one launch (start us, length us, event | category | flops | bytes accessed | tf_op | source)
XLA Modules:
  0.0 63.1 jit_solution(17889776408995407359)
XLA Ops:
  0.6 59.1 %lanczos.1 = (f32[4,24,384]{2,1,0:T(8,128)}, f32[1,1]{1,0:T(1,128)}) custom-call(bf16[13,8,576]{2,1,0:T(8,128)(2,1)} %bitcast.13, bf16[13,8,576]{2,1,0:T(8,128)(2,1)} %bitcast.14, s32[1,128]{1,0:T(1,128)} %slot_in.1, f32[4,576]{1,0:T(4,128)} %bitcast.15, f32[4,24,384]{2,1,0:T(8,128)} %bitcast.11, bf16[13,256]{1,0:T(8,128)(2,1)} %bitcast.16, s32[1,4]{1,0:T(1,128)} %kept_in.1), custom_call_target="tpu_custom_call" | custom-call | tf_op jit(solution)/shard_map/lanczos/pallas_call | solution.py:363
  59.7 1.6 %copy.11 = f32[1,4,24,384]{3,2,1,0:T(8,128)} copy(f32[1,4,24,384]{3,2,1,0:T(8,128)} %bitcast.12) | data formatting | bytes 294912

commit v5 on v4

--- a/solution.py
+++ b/solution.py
@@ -262,11 +262,12 @@
         for w in range(NW):
             h = mixed[0, :, 16 * w:16 * w + 16, :].reshape(384, 128)
             lo = mixed[1, :, 16 * w:16 * w + 16, :].reshape(384, 128)
-            moved[w] = jnp.dot(jnp.concatenate([h, lo], 1), c2[w], preferred_element_type=F)
+            o = jnp.dot(jnp.concatenate([h, lo], 1), c2[w], preferred_element_type=F)
+            moved[w] = jnp.swapaxes(o.reshape(NB, NP, 128), 0, 1)
 
     def left_step(k, a2):
         for q in range(0, NP, 2):
-            r = jnp.concatenate([jnp.concatenate([moved[w, pl.ds(q + j, NB, stride=NP), :] for w in range(NW)], 0) for j in range(2)], 1)
+            r = jnp.concatenate([jnp.concatenate([moved[w, q + j] for w in range(NW)], 0) for j in range(2)], 1)
             h = r.astype(H).astype(F)
             o = jnp.dot(a2, jnp.concatenate([h, r - h], 0).astype(H), preferred_element_type=F)
             for j in range(2):
@@ -324,8 +325,9 @@
     r8 = lax.broadcasted_iota(jnp.int32, (8, 128), 0)
     lhs = jnp.where(r8 == 0, 1.0, jnp.where((r8 == 1) & keep, 1.0, 0.0))
     s = lax.dot_general(lhs, g, (((1,), (1,)), ((), ())), precision=lax.Precision.HIGHEST, preferred_element_type=F)
+    s = s[0:1] + pltpu.roll(s[1:2], 64, 1)
     for i, val in enumerate([n0] + alphas + betas):
-        s = s + jnp.where((lane == 16 + i) & (r8 == 0), val, 0.0)
+        s = s + jnp.where(lane == 16 + i, val, 0.0)
     st[...] = s
 
     def qcopy(j):
@@ -338,8 +340,7 @@
     loop(1, nsec, lambda j: qcopy(j).wait())
     z = jnp.zeros((128 - nsec, 128), F)
     q0 = jnp.concatenate([strecv[:, 0, :], z], 0).T
-    q1 = jnp.concatenate([strecv[:, 1, :], z], 0).T
-    e, f = global_solve(lambda i: q0[i:i + 1, :], lambda i: q1[i:i + 1, :], entries)
+    e, f = global_solve(lambda i: q0[i:i + 1, :], lambda i: q0[64 + i:65 + i, :], entries)
     en_ref[...] = e
     mine = [jnp.sum(jnp.where(lane == me, c, 0.0), axis=1, keepdims=True) for c in f]
     y = mine[0] * v_ref[0]
@@ -382,25 +383,27 @@
             pltpu.VMEM((nsec, 64, 128), H),
             pltpu.VMEM((nch, NT, 576), F),
             pltpu.VMEM((5, 384, 128), F),
-            pltpu.VMEM((8, 128), F),
-            pltpu.VMEM((nsec, 8, 128), F),
+            pltpu.VMEM((1, 128), F),
+            pltpu.VMEM((nsec, 1, 128), F),
             pltpu.VMEM((16, 640), F),
             pltpu.VMEM((1024, 128), F),
             pltpu.VMEM((1664, 128), F),
             pltpu.VMEM((208, 32), H),
             pltpu.VMEM((NW, 256, 128), H),
             pltpu.VMEM((2, NB, 208, 128), H),
-            pltpu.VMEM((NW, 384, 128), F),
+            pltpu.VMEM((NW, NP, NB, 128), F),
             pltpu.VMEM((384, 128), F),
             pltpu.VMEM((384, 128), F),
             dma((2, nsec)), dma((2, nsec)), dma((nch,)), dma((nch,)), dma((nsec,)), dma((nsec,)),
         ],
-        compiler_params=pltpu.CompilerParams(collective_id=0, has_side_effects=True, vmem_limit_bytes=64 * 2**20),
+        compiler_params=pltpu.CompilerParams(collective_id=0, has_side_effects=True, vmem_limit_bytes=48 * 2**20),
         name="lanczos",
-    )(
-        jnp.swapaxes(left_env[0], 0, 1), jnp.swapaxes(right_env[0], 0, 1), env_slot, transfer[0], wavefunction[0],
-        pair_ops[0], kept_ranks,
-    )
+    )(*(
+        pltpu.with_memory_space_constraint(a, pltpu.HBM)
+        for a in (
+            jnp.swapaxes(left_env[0], 0, 1), jnp.swapaxes(right_env[0], 0, 1), env_slot, transfer[0], wavefunction[0],
+            pair_ops[0], kept_ranks)
+    ))
     return out[None], en.reshape(1)
 
 

time: 63.2 us -> 59.4 us (0.940)
  Pallas kernels: 59.1 us -> 56.2 us
  local copies, waits for them, and re-layouts: 1.58 us -> 0.66 us
    pallas_call x1, Pallas kernels: 59.1 us -> 56.2 us  [body(): pl.pallas_call(functools.partial(whole, entries, nsec, nch), out_shape=(j...]
    unnamed x1, local copies, waits for them, and re-layouts: 1.58 us -> 0.66 us
where the time goes in v5:
time: 59.4 us; the launch traced here: 59.2 us
  Pallas kernels  56.2 us (95%)
  between operations  2.33 us (4%)
  local copies, waits for them, and re-layouts  0.66 us (1%)
    pallas_call x1, Pallas kernels, body(): pl.pallas_call(functools.partial(whole, entries, nsec, nch), out_shape=(j...  56.2 us

profile of v5, /device:TPU:4, one launch (start us, length us, event | category | flops | bytes accessed | tf_op | source)
XLA Modules:
  0.0 59.2 jit_solution(13955670382575666164)
XLA Ops:
  0.6 56.2 %lanczos.1 = (f32[4,24,384]{2,1,0:T(8,128)S(1)}, f32[1,1]{1,0:T(1,128)}) custom-call(bf16[13,8,576]{2,1,0:T(8,128)(2,1)} %bitcast.13, bf16[13,8,576]{2,1,0:T(8,128)(2,1)} %bitcast.14, s32[1,128]{1,0:T(1,128)} %slot_in.1, f32[4,576]{1,0:T(4,128)} %bitcast.15, f32[4,24,384]{2,1,0:T(8,128)} %bitcast.12, bf16[13,256]{1,0:T(8,128)(2,1)} %bitcast.16, s32[1,4]{1,0:T(1,128)} %kept_in.1), custom_call_target="tpu_custom_call" | custom-call | tf_op jit(solution)/shard_map/lanczos/pallas_call | solution.py:364
  56.9 0.7 %copy.11 = f32[1,4,24,384]{3,2,1,0:T(8,128)} copy(f32[1,4,24,384]{3,2,1,0:T(8,128)S(1)} %bitcast.11) | data formatting | bytes 294912

commit v6 on v5

--- a/solution.py
+++ b/solution.py
@@ -49,78 +49,115 @@
     lax.fori_loop(a, b, step, 0)
 
 
-def global_solve(q0,q1,entries):
-    tot=lambda x: jnp.sum(x,axis=1,keepdims=True)
-    pos={}
-    n=0
+def total(x):
+    return jnp.sum(x, axis=1, keepdims=True)
+
+
+def weighted(m, a, b):
+    acc = None
+    for i in range(len(a)):
+        s = None
+        for j in range(len(b)):
+            z = m[i][j] * b[j]
+            s = z if s is None else s + z
+        s = s * a[i]
+        acc = s if acc is None else acc + s
+    return acc
+
+
+def recursion(q, sel):
+    pos = {}
     for i in range(4):
-        for j in range(i,5):
-            pos[i,j]=n; n+=1
-    M=[[q0(pos[min(i,j),max(i,j)]) for j in range(4)] for i in range(4)]
-    Mk=[[q1(pos[min(i,j),max(i,j)]) for j in range(4)] for i in range(4)]
-    Wv=[q0(pos[i,4]) for i in range(4)]
-    n0=q0(16); al=[q0(17+i) for i in range(3)]; be=[q0(20+i) for i in range(3)]
-    def tmul(c):
-        k=len(c)-1
-        y=[None]*min(k+2,4)
-        def add(i,z):
-            y[i]=z if y[i] is None else y[i]+z
-        for j in range(min(k+1,3)):
-            add(j,al[j]*c[j]); add(j+1,be[j]*c[j])
-            if j>0: add(j-1,be[j-1]*c[j])
+        for j in range(i, 4):
+            pos[i, j] = pos[j, i] = len(set(pos.values()))
+    gram = [[q(pos[i, j]) for j in range(4)] for i in range(4)]
+    kept = [[q(64 + pos[i, j]) for j in range(4)] for i in range(4)]
+    n0 = q(16)
+    al = [q(17 + i) for i in range(3)]
+    be = [q(20 + i) for i in range(3)]
+
+    def image(c):
+        k = len(c) - 1
+        y = [None] * min(k + 2, 4)
+
+        def add(i, z):
+            y[i] = z if y[i] is None else y[i] + z
+
+        for j in range(min(k + 1, 3)):
+            add(j, al[j] * c[j])
+            add(j + 1, be[j] * c[j])
+            if j > 0:
+                add(j - 1, be[j - 1] * c[j])
         return y
-    def dot(Mx,a,b):
-        acc=None
-        for i in range(len(a)):
-            s=None
-            for j in range(len(b)):
-                z=Mx[i][j]*b[j]; s=z if s is None else s+z
-            s=s*a[i]; acc=s if acc is None else acc+s
-        return acc
-    c=[n0/jnp.sqrt(tot(n0*n0))]
-    cp=[]; b=None
-    cs=[]; A=[]; Bt=[]
+
+    c = [n0 / jnp.sqrt(total(n0 * n0))]
+    cp = []
+    b = None
+    cs = []
+    diag = []
+    off = []
     for k in range(4):
         cs.append(c)
-        y=tmul(c)
-        g=dot(M,c,y)
-        if k==3:
-            s=None
-            for i in range(4):
-                z=c[i]*Wv[i]; s=z if s is None else s+z
-            g=g+s*c[3]
-        a=tot(g); A.append(a)
-        if k<3:
-            r=[]
-            for i in range(len(y)):
-                z=y[i]
-                if i<len(c): z=z-a*c[i]
-                if i<len(cp): z=z-b*cp[i]
-                r.append(z)
-            b=jnp.sqrt(tot(dot(M,r,r))); Bt.append(b)
-            cp=c; c=[z/b for z in r]
-    ab=[jnp.abs(z) for z in Bt]
-    bounds=[A[0]-ab[0],A[1]-ab[0]-ab[1],A[2]-ab[1]-ab[2],A[3]-ab[2]]
-    init=jnp.minimum(jnp.minimum(bounds[0],bounds[1]),jnp.minimum(bounds[2],bounds[3]))-1.0
-    B2=[z*z for z in Bt]
-    def newton(_,e):
-        vp=jnp.ones_like(e); vn=A[0]-e; sp=jnp.zeros_like(e); sn=-jnp.ones_like(e)
-        for p in range(1,4):
-            sh=A[p]-e; w=B2[p-1]
-            v2=sh*vn-w*vp; s2=sh*sn-vn-w*sp
-            vp,vn=vn,v2; sp,sn=sn,s2
-        return e-vn/sn
-    e=lax.fori_loop(0,40,newton,init)
-    co=[jnp.ones_like(e),(e-A[0])/Bt[0]]
-    for p in range(1,3):
-        co.append(((e-A[p])*co[p]-Bt[p-1]*co[p-1])/Bt[p])
-    nrm=jnp.sqrt(co[0]*co[0]+co[1]*co[1]+co[2]*co[2]+co[3]*co[3])
-    f=[None]*4
-    for k in range(4):
-        for i in range(len(cs[k])):
-            z=(co[k]/nrm)*cs[k][i]; f[i]=z if f[i] is None else f[i]+z
-    scale=jnp.sqrt(entries/tot(dot(Mk,f,f)))
-    return e,[z*scale for z in f]
+        y = image(c)
+        g = weighted(gram, c, y)
+        if k == 3:
+            break
+        a = total(g)
+        diag.append(a)
+        r = []
+        for i in range(len(y)):
+            z = y[i]
+            if i < len(c):
+                z = z - a * c[i]
+            if i < len(cp):
+                z = z - b * cp[i]
+            r.append(z)
+        b = jnp.sqrt(total(weighted(gram, r, r)))
+        off.append(b)
+        cp = c
+        c = [z / b for z in r]
+    norms = [[total(weighted(kept, cs[k], cs[m])) for m in range(4)] for k in range(4)]
+    mine = [[total(jnp.where(sel, z, 0.0)) for z in cs[k]] for k in range(4)]
+    return cs, g, diag, off, norms, mine
+
+
+def smallest(d, off):
+    ab = [jnp.abs(z) for z in off]
+    w2 = [z * z for z in off]
+    least = lambda v: jnp.minimum(jnp.minimum(v[0], v[1]), jnp.minimum(v[2], v[3]))
+    lo = least([d[0] - ab[0], d[1] - ab[0] - ab[1], d[2] - ab[1] - ab[2], d[3] - ab[2]])
+    hi = least(d)
+    idx = (lax.broadcasted_iota(jnp.int32, (8, 128), 0) * 128 + lax.broadcasted_iota(jnp.int32, (8, 128), 1) + 1).astype(F)
+    for _ in range(2):
+        h = (hi - lo) * (1.0 / 1024.0)
+        x = lo + h * idx
+        p1 = d[0] - x
+        p2 = (d[1] - x) * p1 - w2[0]
+        p3 = (d[2] - x) * p2 - w2[1] * p1
+        p4 = (d[3] - x) * p3 - w2[2] * p2
+        below = (p1 > 0) & (p2 > 0) & (p3 > 0) & (p4 > 0)
+        x = jnp.where(below, x, lo)
+        lo = jnp.max(jnp.max(x, axis=0, keepdims=True), axis=1, keepdims=True)
+        hi = lo + h
+    e = lo
+    for _ in range(3):
+        vp, vn, sp, sn = jnp.ones_like(e), d[0] - e, jnp.zeros_like(e), -jnp.ones_like(e)
+        for p in range(1, 4):
+            z = d[p] - e
+            v2 = z * vn - w2[p - 1] * vp
+            s2 = z * sn - vn - w2[p - 1] * sp
+            vp, vn, sp, sn = vn, v2, sn, s2
+        e = e - jnp.where(sn != 0, vn / sn, 0.0)
+    return e
+
+
+def ritz(d, off):
+    e = smallest(d, off)
+    co = [jnp.ones_like(e), (e - d[0]) / off[0]]
+    for p in range(1, 3):
+        co.append(((e - d[p]) * co[p] - off[p - 1] * co[p - 1]) / off[p])
+    n = jnp.sqrt(co[0] * co[0] + co[1] * co[1] + co[2] * co[2] + co[3] * co[3])
+    return e, [z / n for z in co]
 
 
 def whole(
@@ -128,8 +165,8 @@
     left_in, right_in, slot_in, tr_in, x_in, b_in, kept_in,
     out_ref, en_ref,
     left, right, slot_ref, tr, x_ref, b_ref, kept_ref, lsem,
-    wide, wire, cat, stage, recv0, recv1, trecv, v_ref, st, strecv,
-    tpad, tbd, ebd, b2, c2, mixed, moved, acat, ybuf,
+    wide, wire, cat, stage, recv0, recv1, trecv, v_ref, st, strecv0, strecv1, vout,
+    tpad, tbd, ebd, b2, c2, mixed, moved, acat,
     ssem, rsem, tssem, trsem, qssem, qrsem,
 ):
     me = lax.axis_index("sector")
@@ -300,57 +337,87 @@
 
     alphas = []
     betas = []
-    for k in range(4):
+    for k in range(3):
         if k > 0:
             pair_step(k)
             right_step()
         left_step(k, a2)
-        if k < 3:
-            y = v_ref[k + 1]
-            a = full(v_ref[k] * y)
-            r = y - a * v_ref[k]
-            if k > 0:
-                r = r - betas[-1] * v_ref[k - 1]
-            b = jnp.sqrt(full(r * r))
-            alphas.append(a)
-            betas.append(b)
-            v_ref[k + 1] = r * inverse(b)
-    rows = []
-    for i in range(4):
-        for j in range(i, 5):
-            rows.append(jnp.sum(v_ref[i] * v_ref[j], axis=0, keepdims=True))
-    g = jnp.concatenate(rows + [jnp.zeros((114, 128), F)], 0)
+        y = v_ref[k + 1]
+        a = full(v_ref[k] * y)
+        r = y - a * v_ref[k]
+        if k > 0:
+            r = r - betas[-1] * v_ref[k - 1]
+        b = jnp.sqrt(full(r * r))
+        alphas.append(a)
+        betas.append(b)
+        v_ref[k + 1] = r * inverse(b)
+
+    def qcopy(i, j):
+        return pltpu.make_async_remote_copy(
+            src_ref=st.at[i], dst_ref=(strecv0, strecv1)[i].at[me], send_sem=qssem.at[i, j], recv_sem=qrsem.at[i, j],
+            device_id=(ch, lax.rem(me + j, nsec)), device_id_type=MESH)
+
+    def lanes(rows):
+        g = jnp.concatenate(rows + [jnp.zeros((128 - len(rows), 128), F)], 0)
+        return lax.dot_general(lhs, g, (((1,), (1,)), ((), ())), precision=lax.Precision.HIGHEST, preferred_element_type=F)
+
+    def gathered(ref):
+        return jnp.concatenate([ref[:, 0, :], jnp.zeros((128 - nsec, 128), F)], 0).T
+
     kp = jnp.where(tl == 0, kept_ref[0, 0], jnp.where(tl == 1, kept_ref[0, 1], jnp.where(tl == 2, kept_ref[0, 2], kept_ref[0, 3])))
     keep = lax.rem(lane, 32) < kp
     r8 = lax.broadcasted_iota(jnp.int32, (8, 128), 0)
     lhs = jnp.where(r8 == 0, 1.0, jnp.where((r8 == 1) & keep, 1.0, 0.0))
-    s = lax.dot_general(lhs, g, (((1,), (1,)), ((), ())), precision=lax.Precision.HIGHEST, preferred_element_type=F)
+    s = lanes([jnp.sum(v_ref[i] * v_ref[j], axis=0, keepdims=True) for i in range(4) for j in range(i, 4)])
     s = s[0:1] + pltpu.roll(s[1:2], 64, 1)
     for i, val in enumerate([n0] + alphas + betas):
         s = s + jnp.where(lane == 16 + i, val, 0.0)
-    st[...] = s
-
-    def qcopy(j):
-        return pltpu.make_async_remote_copy(
-            src_ref=st, dst_ref=strecv.at[me], send_sem=qssem.at[j], recv_sem=qrsem.at[j],
-            device_id=(ch, lax.rem(me + j, nsec)), device_id_type=MESH)
-
-    loop(1, nsec, lambda j: qcopy(j).start())
-    strecv[me] = s
-    loop(1, nsec, lambda j: qcopy(j).wait())
-    z = jnp.zeros((128 - nsec, 128), F)
-    q0 = jnp.concatenate([strecv[:, 0, :], z], 0).T
-    e, f = global_solve(lambda i: q0[i:i + 1, :], lambda i: q0[64 + i:65 + i, :], entries)
+    st[0] = s
+    loop(1, nsec, lambda j: qcopy(0, j).start())
+    strecv0[me] = s
+    pair_step(3)
+    right_step()
+    left_step(3, a2)
+    s = lanes([jnp.sum(v_ref[i] * v_ref[4], axis=0, keepdims=True) for i in range(4)])[0:1]
+    st[1] = s
+    loop(1, nsec, lambda j: qcopy(1, j).start())
+    strecv1[me] = s
+    for k in range(1, 4):
+        for p in range(NP):
+            a = v_ref[k, pl.ds(p, NB, stride=NP), :]
+            for t in range(NT):
+                vout[k - 1, t, :, NB * p:NB * p + NB] = a[:, 32 * t:32 * t + NB]
+    loop(1, nsec, lambda j: qcopy(0, j).wait())
+    q0 = gathered(strecv0)
+    cs, g, diag, off, norms, mine = recursion(lambda i: q0[i:i + 1, :], lane == me)
+    loop(1, nsec, lambda j: qcopy(1, j).wait())
+    q1 = gathered(strecv1)
+    z = cs[3][0] * q1[0:1, :]
+    for i in range(1, 4):
+        z = z + cs[3][i] * q1[i:i + 1, :]
+    diag.append(total(g + z * cs[3][3]))
+    e, co = ritz(diag, off)
     en_ref[...] = e
-    mine = [jnp.sum(jnp.where(lane == me, c, 0.0), axis=1, keepdims=True) for c in f]
-    y = mine[0] * v_ref[0]
-    for i in range(1, 4):
-        y = y + mine[i] * v_ref[i]
-    ybuf[...] = jnp.where(keep, y, 0.0)
-    for p in range(NP):
-        a = ybuf[pl.ds(p, NB, stride=NP), :]
-        for t in range(NT):
-            out_ref[t, :, NB * p:NB * p + NB] = a[:, 32 * t:32 * t + NB]
+    n2 = None
+    for k in range(4):
+        for m in range(4):
+            z = co[k] * co[m] * norms[k][m]
+            n2 = z if n2 is None else n2 + z
+    scale = jnp.sqrt(entries / n2)
+    f = []
+    for i in range(4):
+        z = None
+        for k in range(i, 4):
+            c = co[k] * mine[k][i]
+            z = c if z is None else z + c
+        f.append(z * scale)
+    f[0] = f[0] * inverse(n0)
+    column = lax.rem(lax.broadcasted_iota(jnp.int32, (1, NP * NB), 1), NB)
+    for t in range(NT):
+        y = f[0] * x_ref[t]
+        for k in range(1, 4):
+            y = y + f[k] * vout[k - 1, t]
+        out_ref[t] = jnp.where(column < kept_ref[0, t], y, 0.0)
 
 
 def body(wavefunction, transfer, left_env, right_env, pair_ops, env_slot, kept_ranks):
@@ -383,8 +450,10 @@
             pltpu.VMEM((nsec, 64, 128), H),
             pltpu.VMEM((nch, NT, 576), F),
             pltpu.VMEM((5, 384, 128), F),
-            pltpu.VMEM((1, 128), F),
+            pltpu.VMEM((2, 1, 128), F),
             pltpu.VMEM((nsec, 1, 128), F),
+            pltpu.VMEM((nsec, 1, 128), F),
+            pltpu.VMEM((3, NT, NB, NP * NB), F),
             pltpu.VMEM((16, 640), F),
             pltpu.VMEM((1024, 128), F),
             pltpu.VMEM((1664, 128), F),
@@ -393,8 +462,7 @@
             pltpu.VMEM((2, NB, 208, 128), H),
             pltpu.VMEM((NW, NP, NB, 128), F),
             pltpu.VMEM((384, 128), F),
-            pltpu.VMEM((384, 128), F),
-            dma((2, nsec)), dma((2, nsec)), dma((nch,)), dma((nch,)), dma((nsec,)), dma((nsec,)),
+            dma((2, nsec)), dma((2, nsec)), dma((nch,)), dma((nch,)), dma((2, nsec)), dma((2, nsec)),
         ],
         compiler_params=pltpu.CompilerParams(collective_id=0, has_side_effects=True, vmem_limit_bytes=48 * 2**20),
         name="lanczos",

time: 59.4 us -> 58.7 us (0.988)
  Pallas kernels: 56.2 us -> 55.6 us
    pallas_call x1, Pallas kernels: 56.2 us -> 55.6 us  [body(): pl.pallas_call(functools.partial(whole, entries, nsec, nch), out_shape=(j...]
where the time goes in v6:
time: 58.7 us; the launch traced here: 58.6 us
  Pallas kernels  55.6 us (95%)
  between operations  2.33 us (4%)
  local copies, waits for them, and re-layouts  0.66 us (1%)
    pallas_call x1, Pallas kernels, body(): pl.pallas_call(functools.partial(whole, entries, nsec, nch), out_shape=(j...  55.6 us

profile of v6, /device:TPU:4, one launch (start us, length us, event | category | flops | bytes accessed | tf_op | source)
XLA Modules:
  0.0 58.6 jit_solution(9547296337777849878)
XLA Ops:
  0.6 55.6 %lanczos.1 = (f32[4,24,384]{2,1,0:T(8,128)S(1)}, f32[1,1]{1,0:T(1,128)}) custom-call(bf16[13,8,576]{2,1,0:T(8,128)(2,1)} %bitcast.13, bf16[13,8,576]{2,1,0:T(8,128)(2,1)} %bitcast.14, s32[1,128]{1,0:T(1,128)} %slot_in.1, f32[4,576]{1,0:T(4,128)} %bitcast.15, f32[4,24,384]{2,1,0:T(8,128)} %bitcast.12, bf16[13,256]{1,0:T(8,128)(2,1)} %bitcast.16, s32[1,4]{1,0:T(1,128)} %kept_in.1), custom_call_target="tpu_custom_call" | custom-call | tf_op jit(solution)/shard_map/lanczos/pallas_call | solution.py:431
  56.3 0.7 %copy.11 = f32[1,4,24,384]{3,2,1,0:T(8,128)} copy(f32[1,4,24,384]{3,2,1,0:T(8,128)S(1)} %bitcast.11) | data formatting | bytes 294912

commit v7 on v6

--- a/solution.py
+++ b/solution.py
@@ -166,7 +166,7 @@
     out_ref, en_ref,
     left, right, slot_ref, tr, x_ref, b_ref, kept_ref, lsem,
     wide, wire, cat, stage, recv0, recv1, trecv, v_ref, st, strecv0, strecv1, vout,
-    tpad, tbd, ebd, b2, c2, mixed, moved, acat,
+    tpad, tbd, ebd, b2, c2, c1, mixed, moved, acat,
     ssem, rsem, tssem, trsem, qssem, qrsem,
 ):
     me = lax.axis_index("sector")
@@ -209,8 +209,14 @@
 
     def ecopy(side, j):
         return pltpu.make_async_remote_copy(
-            src_ref=stage.at[side, j], dst_ref=(recv0, recv1)[side].at[j], send_sem=ssem.at[side, j], recv_sem=rsem.at[side, j],
+            src_ref=stage.at[side, j], dst_ref=(recv0, recv1)[side].at[j], send_sem=ssem.at[side], recv_sem=rsem.at[side],
             device_id=(ch, lax.rem(me + j, nsec)), device_id_type=MESH)
+
+    def everyone(ref, send_sem, recv_sem):
+        rows = ref.at[pl.ds(1, nsec - 1)]
+        return pltpu.make_async_remote_copy(
+            src_ref=rows, dst_ref=rows, send_sem=send_sem, recv_sem=recv_sem,
+            device_id=(ch, lax.rem(me + 1, nsec)), device_id_type=MESH)
 
     loads[0].wait()
     chosen = []
@@ -272,6 +278,7 @@
     ph, plo = split(pre.T)
 
     ebd[...] = jnp.zeros_like(ebd)
+    c1[...] = jnp.zeros_like(c1)
 
     def spread(side):
         for t in range(NT):
@@ -283,7 +290,7 @@
             for i in range(NB):
                 ebd[pl.ds(32 * t + i, NW, stride=128), :] = grab(tile, NB * i, t, lane)
 
-    def pair_step(k):
+    def pair_step(k, parts=2):
         bm = b2[...]
         for l in range(0, NB, 2):
             xx = jnp.concatenate([v_ref[k, 16 * l:16 * l + 16, :], v_ref[k, 16 * l + 16:16 * l + 32, :]], 1)
@@ -292,8 +299,9 @@
             h, lo = split(o)
             mixed[0, l] = h[:, :128]
             mixed[0, l + 1] = h[:, 128:]
-            mixed[1, l] = lo[:, :128]
-            mixed[1, l + 1] = lo[:, 128:]
+            if parts == 2:
+                mixed[1, l] = lo[:, :128]
+                mixed[1, l + 1] = lo[:, 128:]
 
     def right_step():
         for w in range(NW):
@@ -302,18 +310,28 @@
             o = jnp.dot(jnp.concatenate([h, lo], 1), c2[w], preferred_element_type=F)
             moved[w] = jnp.swapaxes(o.reshape(NB, NP, 128), 0, 1)
 
-    def left_step(k, a2):
+    def right_step_rounded():
+        for w in range(0, NW, 2):
+            n = min(2, NW - w)
+            h = jnp.concatenate([mixed[0, :, 16 * (w + i):16 * (w + i) + 16, :].reshape(384, 128) for i in range(n)], 1)
+            o = jnp.dot(h, c1[w // 2, 0:128 * n, 0:128 * n], preferred_element_type=F)
+            for i in range(n):
+                moved[w + i] = jnp.swapaxes(o[:, 128 * i:128 * i + 128].reshape(NB, NP, 128), 0, 1)
+
+    def left_step(k, a2, parts=2):
         for q in range(0, NP, 2):
             r = jnp.concatenate([jnp.concatenate([moved[w, q + j] for w in range(NW)], 0) for j in range(2)], 1)
-            h = r.astype(H).astype(F)
-            o = jnp.dot(a2, jnp.concatenate([h, r - h], 0).astype(H), preferred_element_type=F)
+            if parts == 2:
+                h = r.astype(H).astype(F)
+                r = jnp.concatenate([h, r - h], 0)
+            o = jnp.dot(a2[:, :312 * parts], r.astype(H), preferred_element_type=F)
             for j in range(2):
                 oj = o[:, 128 * j:128 * j + 128]
                 y = jnp.where(tl == 0, oj[0:24], jnp.where(tl == 1, oj[24:48], jnp.where(tl == 2, oj[48:72], oj[72:96])))
                 v_ref[k + 1, pl.ds(q + j, NB, stride=NP), :] = y
 
     pair_step(0)
-    loop(1, nsec, lambda j: ecopy(1, j).wait())
+    everyone(recv1, ssem.at[1], rsem.at[1]).wait()
     spread(1)
     pp = jnp.concatenate([ph, plo], 0)
     pq = jnp.concatenate([ph, plo, ph], 0)
@@ -327,12 +345,14 @@
     al = acat[...].T
     al = jnp.concatenate([al[32 * t:32 * t + 24] for t in range(NT)], 0)[:, :312].astype(H).astype(F)
     a2 = jnp.concatenate([al, al], 1).astype(H)
-    loop(1, nsec, lambda j: ecopy(0, j).wait())
+    everyone(recv0, ssem.at[0], rsem.at[0]).wait()
     spread(0)
     for w in range(NW):
         ct = ebd[w * 128:(w + 1) * 128, :].T.astype(H)
         c2[w, 0:128, :] = ct
         c2[w, 128:256, :] = ct
+        i = 128 * (w % 2)
+        c1[w // 2, i:i + 128, i:i + 128] = ct
     right_step()
 
     alphas = []
@@ -354,7 +374,7 @@
 
     def qcopy(i, j):
         return pltpu.make_async_remote_copy(
-            src_ref=st.at[i], dst_ref=(strecv0, strecv1)[i].at[me], send_sem=qssem.at[i, j], recv_sem=qrsem.at[i, j],
+            src_ref=st.at[i], dst_ref=(strecv0, strecv1)[i].at[j], send_sem=qssem.at[i], recv_sem=qrsem.at[i],
             device_id=(ch, lax.rem(me + j, nsec)), device_id_type=MESH)
 
     def lanes(rows):
@@ -373,24 +393,26 @@
     for i, val in enumerate([n0] + alphas + betas):
         s = s + jnp.where(lane == 16 + i, val, 0.0)
     st[0] = s
-    loop(1, nsec, lambda j: qcopy(0, j).start())
-    strecv0[me] = s
-    pair_step(3)
-    right_step()
-    left_step(3, a2)
+    for j in range(1, nsec):
+        qcopy(0, j).start()
+    strecv0[0] = s
+    pair_step(3, 1)
+    right_step_rounded()
+    left_step(3, a2, 1)
     s = lanes([jnp.sum(v_ref[i] * v_ref[4], axis=0, keepdims=True) for i in range(4)])[0:1]
     st[1] = s
-    loop(1, nsec, lambda j: qcopy(1, j).start())
-    strecv1[me] = s
+    for j in range(1, nsec):
+        qcopy(1, j).start()
+    strecv1[0] = s
     for k in range(1, 4):
         for p in range(NP):
             a = v_ref[k, pl.ds(p, NB, stride=NP), :]
             for t in range(NT):
                 vout[k - 1, t, :, NB * p:NB * p + NB] = a[:, 32 * t:32 * t + NB]
-    loop(1, nsec, lambda j: qcopy(0, j).wait())
+    everyone(strecv0, qssem.at[0], qrsem.at[0]).wait()
     q0 = gathered(strecv0)
-    cs, g, diag, off, norms, mine = recursion(lambda i: q0[i:i + 1, :], lane == me)
-    loop(1, nsec, lambda j: qcopy(1, j).wait())
+    cs, g, diag, off, norms, mine = recursion(lambda i: q0[i:i + 1, :], lane == 0)
+    everyone(strecv1, qssem.at[1], qrsem.at[1]).wait()
     q1 = gathered(strecv1)
     z = cs[3][0] * q1[0:1, :]
     for i in range(1, 4):
@@ -459,10 +481,11 @@
             pltpu.VMEM((1664, 128), F),
             pltpu.VMEM((208, 32), H),
             pltpu.VMEM((NW, 256, 128), H),
+            pltpu.VMEM(((NW + 1) // 2, 256, 256), H),
             pltpu.VMEM((2, NB, 208, 128), H),
             pltpu.VMEM((NW, NP, NB, 128), F),
             pltpu.VMEM((384, 128), F),
-            dma((2, nsec)), dma((2, nsec)), dma((nch,)), dma((nch,)), dma((2, nsec)), dma((2, nsec)),
+            dma((2,)), dma((2,)), dma((nch,)), dma((nch,)), dma((2,)), dma((2,)),
         ],
         compiler_params=pltpu.CompilerParams(collective_id=0, has_side_effects=True, vmem_limit_bytes=48 * 2**20),
         name="lanczos",

time: 58.7 us -> 55.7 us (0.949)
  Pallas kernels: 55.6 us -> 52.6 us
    pallas_call x1, Pallas kernels: 55.6 us -> 52.6 us  [body(): pl.pallas_call(functools.partial(whole, entries, nsec, nch), out_shape=(j...]
where the time goes in v7:
time: 55.7 us; the launch traced here: 55.6 us
  Pallas kernels  52.6 us (94%)
  between operations  2.33 us (4%)
  local copies, waits for them, and re-layouts  0.66 us (1%)
    pallas_call x1, Pallas kernels, body(): pl.pallas_call(functools.partial(whole, entries, nsec, nch), out_shape=(j...  52.6 us

profile of v7, /device:TPU:4, one launch (start us, length us, event | category | flops | bytes accessed | tf_op | source)
XLA Modules:
  0.0 55.6 jit_solution(4738509800632206223)
XLA Ops:
  0.6 52.6 %lanczos.1 = (f32[4,24,384]{2,1,0:T(8,128)S(1)}, f32[1,1]{1,0:T(1,128)}) custom-call(bf16[13,8,576]{2,1,0:T(8,128)(2,1)} %bitcast.13, bf16[13,8,576]{2,1,0:T(8,128)(2,1)} %bitcast.14, s32[1,128]{1,0:T(1,128)} %slot_in.1, f32[4,576]{1,0:T(4,128)} %bitcast.15, f32[4,24,384]{2,1,0:T(8,128)} %bitcast.12, bf16[13,256]{1,0:T(8,128)(2,1)} %bitcast.16, s32[1,4]{1,0:T(1,128)} %kept_in.1), custom_call_target="tpu_custom_call" | custom-call | tf_op jit(solution)/shard_map/lanczos/pallas_call | solution.py:453
  53.3 0.7 %copy.11 = f32[1,4,24,384]{3,2,1,0:T(8,128)} copy(f32[1,4,24,384]{3,2,1,0:T(8,128)S(1)} %bitcast.11) | data formatting | bytes 294912

commit v8 on v7

--- a/solution.py
+++ b/solution.py
@@ -165,13 +165,14 @@
     left_in, right_in, slot_in, tr_in, x_in, b_in, kept_in,
     out_ref, en_ref,
     left, right, slot_ref, tr, x_ref, b_ref, kept_ref, lsem,
-    wide, wire, cat, stage, recv0, recv1, trecv, v_ref, st, strecv0, strecv1, vout,
+    wide, wire, cat, stage, recva, recvb, recvl, trecv, v_ref, st, strecv0, strecv1, vout,
     tpad, tbd, ebd, b2, c2, c1, mixed, moved, acat,
     ssem, rsem, tssem, trsem, qssem, qrsem,
 ):
     me = lax.axis_index("sector")
     ch = lax.axis_index("chain")
     cap = left_in.shape[1]
+    recvs = (recva, recvb, recvl)
     lane = lax.broadcasted_iota(jnp.int32, (1, 128), 1)
     tl = lane // 32
     loads = [
@@ -184,20 +185,24 @@
     bar = pltpu.get_barrier_semaphore()
     loop(1, nsec, lambda j: pl.semaphore_signal(bar, inc=1, device_id=(ch, lax.rem(me + j, nsec)), device_id_type=MESH))
     loop(1, nch, lambda j: pl.semaphore_signal(bar, inc=1, device_id=(lax.rem(ch + j, nch), me), device_id_type=MESH))
-    def pack(side, src, chosen):
-        wire[...] = jnp.zeros_like(wire)
+    def widen(src):
         for w in range(NW):
             row8 = src[w].astype(F)
             for c in range(4):
                 wide[c, cap * w:cap * w + cap, :] = row8[:, 128 * c:128 * c + 128]
             wide[4, cap * w:cap * w + cap, 0:64] = row8[:, 512:576]
+
+    def pack(side, row, first, n):
+        half = (n + 1) // 2
         for s in range(cap):
             for c in range(4):
-                wire[s, 13 * c:13 * c + 13, :] = wide[c, pl.ds(s, 13, stride=cap), :]
-            lo = wide[4, pl.ds(s, 7, stride=cap), :]
-            hi = pltpu.roll(wide[4, pl.ds(s + 7 * cap, 6, stride=cap), :], 64, 1)
-            wire[s, 52:59, :] = jnp.where(lane < 64, lo, 0.0)
-            wire[s, 52:58, :] = jnp.where(lane < 64, lo[0:6], hi)
+                wire[s, row + n * c:row + n * c + n, :] = wide[c, pl.ds(s + cap * first, n, stride=cap), :]
+            lo = wide[4, pl.ds(s + cap * first, half, stride=cap), :]
+            hi = pltpu.roll(wide[4, pl.ds(s + cap * (first + half), n - half, stride=cap), :], 64, 1)
+            wire[s, row + 4 * n:row + 4 * n + half, :] = jnp.where(lane < 64, lo, 0.0)
+            wire[s, row + 4 * n:row + 5 * n - half, :] = jnp.where(lane < 64, lo[0:n - half], hi)
+
+    def place(side, chosen):
         cat[side] = wire[...].astype(H)
         for j in range(nsec):
             stage[side, j] = cat[side, chosen[j]]
@@ -207,9 +212,10 @@
             src_ref=tr, dst_ref=trecv.at[ch], send_sem=tssem.at[j], recv_sem=trsem.at[j],
             device_id=(lax.rem(ch + j, nch), me), device_id_type=MESH)
 
-    def ecopy(side, j):
+    def ecopy(part, j):
+        src = stage.at[1, j] if part == 2 else stage.at[0, j, pl.ds(32 * part, 32)]
         return pltpu.make_async_remote_copy(
-            src_ref=stage.at[side, j], dst_ref=(recv0, recv1)[side].at[j], send_sem=ssem.at[side], recv_sem=rsem.at[side],
+            src_ref=src, dst_ref=recvs[part].at[j], send_sem=ssem.at[part], recv_sem=rsem.at[part],
             device_id=(ch, lax.rem(me + j, nsec)), device_id_type=MESH)
 
     def everyone(ref, send_sem, recv_sem):
@@ -228,17 +234,25 @@
             s = s + jnp.where(g // cap == me, lax.rem(g, cap), 0)
         chosen.append(s)
     loads[1].wait()
-    pack(1, left, chosen)
+    wire[...] = jnp.zeros_like(wire)
+    widen(left)
+    pack(1, 0, 0, NW)
+    place(1, chosen)
     loads[2].wait()
     trecv[ch] = tr[...]
     pl.semaphore_wait(bar, nsec + nch - 2)
     loop(1, nch, lambda j: tcopy(j).start())
+    loop(1, nsec, lambda j: ecopy(2, j).start())
+    loads[3].wait()
+    widen(right)
+    pack(0, 0, 0, 7)
+    pack(0, 32, 7, 6)
+    place(0, chosen)
+    loop(1, nsec, lambda j: ecopy(0, j).start())
     loop(1, nsec, lambda j: ecopy(1, j).start())
-    loads[3].wait()
-    pack(0, right, chosen)
-    loop(1, nsec, lambda j: ecopy(0, j).start())
-    recv0[0] = stage[0, 0]
-    recv1[0] = stage[1, 0]
+    recvs[0][0] = stage[0, 0, 0:32]
+    recvs[1][0] = stage[0, 0, 32:64]
+    recvs[2][0] = stage[1, 0]
     loads[4].wait()
     loads[5].wait()
     loads[6].wait()
@@ -280,15 +294,17 @@
     ebd[...] = jnp.zeros_like(ebd)
     c1[...] = jnp.zeros_like(c1)
 
-    def spread(side):
+    def spread(part, first, n):
+        half = (n + 1) // 2
+        m = recvs[part].shape[1]
         for t in range(NT):
             o = slot_ref[0, me * NT + t] // cap
-            wire[t] = (recv0, recv1)[side][lax.rem(me - o + nsec, nsec)].astype(F)
-            tpad[0:7, 0:128] = wire[t, 52:59, :]
-            tpad[7:13, 0:128] = pltpu.roll(wire[t, 52:58, :], 64, 1)
-            tile = lambda c: wire[t, 13 * c:13 * c + 13, :] if c < 4 else tpad[0:13, 0:128]
+            wire[t, 0:m] = recvs[part][lax.rem(me - o + nsec, nsec)].astype(F)
+            tpad[0:half, 0:128] = wire[t, 4 * n:4 * n + half, :]
+            tpad[half:n, 0:128] = pltpu.roll(wire[t, 4 * n:5 * n - half, :], 64, 1)
+            tile = lambda c: wire[t, n * c:n * c + n, :] if c < 4 else tpad[0:n, 0:128]
             for i in range(NB):
-                ebd[pl.ds(32 * t + i, NW, stride=128), :] = grab(tile, NB * i, t, lane)
+                ebd[pl.ds(128 * first + 32 * t + i, n, stride=128), :] = grab(tile, NB * i, t, lane)
 
     def pair_step(k, parts=2):
         bm = b2[...]
@@ -303,8 +319,8 @@
                 mixed[1, l] = lo[:, :128]
                 mixed[1, l + 1] = lo[:, 128:]
 
-    def right_step():
-        for w in range(NW):
+    def right_step(first=0, last=NW):
+        for w in range(first, last):
             h = mixed[0, :, 16 * w:16 * w + 16, :].reshape(384, 128)
             lo = mixed[1, :, 16 * w:16 * w + 16, :].reshape(384, 128)
             o = jnp.dot(jnp.concatenate([h, lo], 1), c2[w], preferred_element_type=F)
@@ -331,8 +347,8 @@
                 v_ref[k + 1, pl.ds(q + j, NB, stride=NP), :] = y
 
     pair_step(0)
-    everyone(recv1, ssem.at[1], rsem.at[1]).wait()
-    spread(1)
+    everyone(recvs[2], ssem.at[2], rsem.at[2]).wait()
+    spread(2, 0, NW)
     pp = jnp.concatenate([ph, plo], 0)
     pq = jnp.concatenate([ph, plo, ph], 0)
     for w in range(NW):
@@ -345,23 +361,27 @@
     al = acat[...].T
     al = jnp.concatenate([al[32 * t:32 * t + 24] for t in range(NT)], 0)[:, :312].astype(H).astype(F)
     a2 = jnp.concatenate([al, al], 1).astype(H)
-    everyone(recv0, ssem.at[0], rsem.at[0]).wait()
-    spread(0)
-    for w in range(NW):
-        ct = ebd[w * 128:(w + 1) * 128, :].T.astype(H)
-        c2[w, 0:128, :] = ct
-        c2[w, 128:256, :] = ct
-        i = 128 * (w % 2)
-        c1[w // 2, i:i + 128, i:i + 128] = ct
-    right_step()
+    for part, first, last in ((0, 0, 7), (1, 7, NW)):
+        everyone(recvs[part], ssem.at[part], rsem.at[part]).wait()
+        spread(part, first, last - first)
+        for w in range(first, last):
+            ct = ebd[w * 128:(w + 1) * 128, :].T.astype(H)
+            c2[w, 0:128, :] = ct
+            c2[w, 128:256, :] = ct
+            i = 128 * (w % 2)
+            c1[w // 2, i:i + 128, i:i + 128] = ct
+        right_step(first, last)
 
     alphas = []
     betas = []
     for k in range(3):
-        if k > 0:
+        if k == 1:
             pair_step(k)
             right_step()
-        left_step(k, a2)
+        if k == 2:
+            pair_step(k, 1)
+            right_step_rounded()
+        left_step(k, a2, 2 if k < 2 else 1)
         y = v_ref[k + 1]
         a = full(v_ref[k] * y)
         r = y - a * v_ref[k]
@@ -468,7 +488,8 @@
             pltpu.VMEM((cap, 64, 128), F),
             pltpu.VMEM((2, cap, 64, 128), H),
             pltpu.VMEM((2, nsec, 64, 128), H),
-            pltpu.VMEM((nsec, 64, 128), H),
+            pltpu.VMEM((nsec, 32, 128), H),
+            pltpu.VMEM((nsec, 32, 128), H),
             pltpu.VMEM((nsec, 64, 128), H),
             pltpu.VMEM((nch, NT, 576), F),
             pltpu.VMEM((5, 384, 128), F),
@@ -485,7 +506,7 @@
             pltpu.VMEM((2, NB, 208, 128), H),
             pltpu.VMEM((NW, NP, NB, 128), F),
             pltpu.VMEM((384, 128), F),
-            dma((2,)), dma((2,)), dma((nch,)), dma((nch,)), dma((2,)), dma((2,)),
+            dma((3,)), dma((3,)), dma((nch,)), dma((nch,)), dma((2,)), dma((2,)),
         ],
         compiler_params=pltpu.CompilerParams(collective_id=0, has_side_effects=True, vmem_limit_bytes=48 * 2**20),
         name="lanczos",

time: 55.7 us -> 54.7 us (0.982)
  Pallas kernels: 52.6 us -> 51.6 us
    pallas_call x1, Pallas kernels: 52.6 us -> 51.6 us  [body(): pl.pallas_call(functools.partial(whole, entries, nsec, nch), out_shape=(j...]
where the time goes in v8:
time: 54.7 us; the launch traced here: 54.6 us
  Pallas kernels  51.6 us (94%)
  between operations  2.33 us (4%)
  local copies, waits for them, and re-layouts  0.66 us (1%)
    pallas_call x1, Pallas kernels, body(): pl.pallas_call(functools.partial(whole, entries, nsec, nch), out_shape=(j...  51.6 us

profile of v8, /device:TPU:4, one launch (start us, length us, event | category | flops | bytes accessed | tf_op | source)
XLA Modules:
  0.0 54.6 jit_solution(3229107987926243261)
XLA Ops:
  0.6 51.6 %lanczos.1 = (f32[4,24,384]{2,1,0:T(8,128)S(1)}, f32[1,1]{1,0:T(1,128)}) custom-call(bf16[13,8,576]{2,1,0:T(8,128)(2,1)} %bitcast.13, bf16[13,8,576]{2,1,0:T(8,128)(2,1)} %bitcast.14, s32[1,128]{1,0:T(1,128)} %slot_in.1, f32[4,576]{1,0:T(4,128)} %bitcast.15, f32[4,24,384]{2,1,0:T(8,128)} %bitcast.12, bf16[13,256]{1,0:T(8,128)(2,1)} %bitcast.16, s32[1,4]{1,0:T(1,128)} %kept_in.1), custom_call_target="tpu_custom_call" | custom-call | tf_op jit(solution)/shard_map/lanczos/pallas_call | solution.py:473
  52.2 0.7 %copy.11 = f32[1,4,24,384]{3,2,1,0:T(8,128)} copy(f32[1,4,24,384]{3,2,1,0:T(8,128)S(1)} %bitcast.11) | data formatting | bytes 294912

commit v9 on v8

--- a/solution.py
+++ b/solution.py
@@ -13,6 +13,7 @@
 NB = 24
 NP = 16
 NW = 13
+NY = 4
 MESH = pl.DeviceIdType.MESH
 
 
@@ -173,6 +174,17 @@
     ch = lax.axis_index("chain")
     cap = left_in.shape[1]
     recvs = (recva, recvb, recvl)
+    my_z, my_y = me // NY, lax.rem(me, NY)
+    nz = nsec // NY
+
+    def peer(j):
+        return lax.rem(my_z + j // NY, nz) * NY + lax.rem(my_y + j % NY, NY)
+
+    def row_of(o):
+        return lax.rem(my_z - o // NY + nz, nz) * NY + lax.rem(my_y - lax.rem(o, NY) + NY, NY)
+
+    far = sorted(range(1, nsec), key=lambda j: -min(j // NY, nz - j // NY) - min(j % NY, NY - j % NY))
+    order = sorted(range(1, nsec), key=lambda j: ((0, 2, 1, 3)[j % NY], -min(j // NY, nz - j // NY)))
     lane = lax.broadcasted_iota(jnp.int32, (1, 128), 1)
     tl = lane // 32
     loads = [
@@ -213,10 +225,10 @@
             device_id=(lax.rem(ch + j, nch), me), device_id_type=MESH)
 
     def ecopy(part, j):
-        src = stage.at[1, j] if part == 2 else stage.at[0, j, pl.ds(32 * part, 32)]
+        src = stage.at[1, j] if part == 2 else stage.at[0, j, pl.ds(48 * part, 48 - 32 * part)]
         return pltpu.make_async_remote_copy(
             src_ref=src, dst_ref=recvs[part].at[j], send_sem=ssem.at[part], recv_sem=rsem.at[part],
-            device_id=(ch, lax.rem(me + j, nsec)), device_id_type=MESH)
+            device_id=(ch, peer(j)), device_id_type=MESH)
 
     def everyone(ref, send_sem, recv_sem):
         rows = ref.at[pl.ds(1, nsec - 1)]
@@ -227,7 +239,7 @@
     loads[0].wait()
     chosen = []
     for j in range(nsec):
-        h = lax.rem(me + j, nsec)
+        h = peer(j)
         s = jnp.int32(0)
         for k in range(NT):
             g = slot_ref[0, h * NT + k]
@@ -242,16 +254,19 @@
     trecv[ch] = tr[...]
     pl.semaphore_wait(bar, nsec + nch - 2)
     loop(1, nch, lambda j: tcopy(j).start())
-    loop(1, nsec, lambda j: ecopy(2, j).start())
+    for j in order:
+        ecopy(2, j).start()
     loads[3].wait()
     widen(right)
-    pack(0, 0, 0, 7)
-    pack(0, 32, 7, 6)
+    pack(0, 0, 0, 10)
+    pack(0, 48, 10, 3)
     place(0, chosen)
-    loop(1, nsec, lambda j: ecopy(0, j).start())
-    loop(1, nsec, lambda j: ecopy(1, j).start())
-    recvs[0][0] = stage[0, 0, 0:32]
-    recvs[1][0] = stage[0, 0, 32:64]
+    for j in order:
+        ecopy(0, j).start()
+    for j in order:
+        ecopy(1, j).start()
+    recvs[0][0] = stage[0, 0, 0:48]
+    recvs[1][0] = stage[0, 0, 48:64]
     recvs[2][0] = stage[1, 0]
     loads[4].wait()
     loads[5].wait()
@@ -299,7 +314,7 @@
         m = recvs[part].shape[1]
         for t in range(NT):
             o = slot_ref[0, me * NT + t] // cap
-            wire[t, 0:m] = recvs[part][lax.rem(me - o + nsec, nsec)].astype(F)
+            wire[t, 0:m] = recvs[part][row_of(o)].astype(F)
             tpad[0:half, 0:128] = wire[t, 4 * n:4 * n + half, :]
             tpad[half:n, 0:128] = pltpu.roll(wire[t, 4 * n:5 * n - half, :], 64, 1)
             tile = lambda c: wire[t, n * c:n * c + n, :] if c < 4 else tpad[0:n, 0:128]
@@ -361,7 +376,7 @@
     al = acat[...].T
     al = jnp.concatenate([al[32 * t:32 * t + 24] for t in range(NT)], 0)[:, :312].astype(H).astype(F)
     a2 = jnp.concatenate([al, al], 1).astype(H)
-    for part, first, last in ((0, 0, 7), (1, 7, NW)):
+    for part, first, last in ((0, 0, 10), (1, 10, NW)):
         everyone(recvs[part], ssem.at[part], rsem.at[part]).wait()
         spread(part, first, last - first)
         for w in range(first, last):
@@ -395,7 +410,7 @@
     def qcopy(i, j):
         return pltpu.make_async_remote_copy(
             src_ref=st.at[i], dst_ref=(strecv0, strecv1)[i].at[j], send_sem=qssem.at[i], recv_sem=qrsem.at[i],
-            device_id=(ch, lax.rem(me + j, nsec)), device_id_type=MESH)
+            device_id=(ch, peer(j)), device_id_type=MESH)
 
     def lanes(rows):
         g = jnp.concatenate(rows + [jnp.zeros((128 - len(rows), 128), F)], 0)
@@ -413,7 +428,7 @@
     for i, val in enumerate([n0] + alphas + betas):
         s = s + jnp.where(lane == 16 + i, val, 0.0)
     st[0] = s
-    for j in range(1, nsec):
+    for j in far:
         qcopy(0, j).start()
     strecv0[0] = s
     pair_step(3, 1)
@@ -421,7 +436,7 @@
     left_step(3, a2, 1)
     s = lanes([jnp.sum(v_ref[i] * v_ref[4], axis=0, keepdims=True) for i in range(4)])[0:1]
     st[1] = s
-    for j in range(1, nsec):
+    for j in far:
         qcopy(1, j).start()
     strecv1[0] = s
     for k in range(1, 4):
@@ -488,8 +503,8 @@
             pltpu.VMEM((cap, 64, 128), F),
             pltpu.VMEM((2, cap, 64, 128), H),
             pltpu.VMEM((2, nsec, 64, 128), H),
-            pltpu.VMEM((nsec, 32, 128), H),
-            pltpu.VMEM((nsec, 32, 128), H),
+            pltpu.VMEM((nsec, 48, 128), H),
+            pltpu.VMEM((nsec, 16, 128), H),
             pltpu.VMEM((nsec, 64, 128), H),
             pltpu.VMEM((nch, NT, 576), F),
             pltpu.VMEM((5, 384, 128), F),

time: 54.7 us -> 53.9 us (0.985)
  Pallas kernels: 51.6 us -> 50.8 us
    pallas_call x1, Pallas kernels: 51.6 us -> 50.8 us  [body(): pl.pallas_call(functools.partial(whole, entries, nsec, nch), out_shape=(j...]
where the time goes in v9:
time: 53.9 us; the launch traced here: 53.8 us
  Pallas kernels  50.8 us (94%)
  between operations  2.33 us (4%)
  local copies, waits for them, and re-layouts  0.66 us (1%)
    pallas_call x1, Pallas kernels, body(): pl.pallas_call(functools.partial(whole, entries, nsec, nch), out_shape=(j...  50.8 us

profile of v9, /device:TPU:4, one launch (start us, length us, event | category | flops | bytes accessed | tf_op | source)
XLA Modules:
  0.0 53.8 jit_solution(14514722708698168452)
XLA Ops:
  0.6 50.8 %lanczos.1 = (f32[4,24,384]{2,1,0:T(8,128)S(1)}, f32[1,1]{1,0:T(1,128)}) custom-call(bf16[13,8,576]{2,1,0:T(8,128)(2,1)} %bitcast.13, bf16[13,8,576]{2,1,0:T(8,128)(2,1)} %bitcast.14, s32[1,128]{1,0:T(1,128)} %slot_in.1, f32[4,576]{1,0:T(4,128)} %bitcast.15, f32[4,24,384]{2,1,0:T(8,128)} %bitcast.12, bf16[13,256]{1,0:T(8,128)(2,1)} %bitcast.16, s32[1,4]{1,0:T(1,128)} %kept_in.1), custom_call_target="tpu_custom_call" | custom-call | tf_op jit(solution)/shard_map/lanczos/pallas_call | solution.py:488
  51.5 0.7 %copy.11 = f32[1,4,24,384]{3,2,1,0:T(8,128)} copy(f32[1,4,24,384]{3,2,1,0:T(8,128)S(1)} %bitcast.11) | data formatting | bytes 294912

commit v10 on v9

--- a/solution.py
+++ b/solution.py
@@ -250,12 +250,12 @@
     widen(left)
     pack(1, 0, 0, NW)
     place(1, chosen)
+    pl.semaphore_wait(bar, nsec + nch - 2)
+    for j in order:
+        ecopy(2, j).start()
     loads[2].wait()
     trecv[ch] = tr[...]
-    pl.semaphore_wait(bar, nsec + nch - 2)
     loop(1, nch, lambda j: tcopy(j).start())
-    for j in order:
-        ecopy(2, j).start()
     loads[3].wait()
     widen(right)
     pack(0, 0, 0, 10)
@@ -390,10 +390,7 @@
     alphas = []
     betas = []
     for k in range(3):
-        if k == 1:
-            pair_step(k)
-            right_step()
-        if k == 2:
+        if k > 0:
             pair_step(k, 1)
             right_step_rounded()
         left_step(k, a2, 2 if k < 2 else 1)
@@ -434,7 +431,9 @@
     pair_step(3, 1)
     right_step_rounded()
     left_step(3, a2, 1)
-    s = lanes([jnp.sum(v_ref[i] * v_ref[4], axis=0, keepdims=True) for i in range(4)])[0:1]
+    s = jnp.zeros((1, 128), F)
+    for i in range(4):
+        s = s + jnp.where(lane == i, full(v_ref[i] * v_ref[4]), 0.0)
     st[1] = s
     for j in far:
         qcopy(1, j).start()

time: 53.9 us -> 53.6 us (level)
  no operation moved by 1% of the time
where the time goes in v10:
time: 53.6 us; the launch traced here: 53.5 us
  Pallas kernels  50.5 us (94%)
  between operations  2.33 us (4%)
  local copies, waits for them, and re-layouts  0.66 us (1%)
    pallas_call x1, Pallas kernels, body(): pl.pallas_call(functools.partial(whole, entries, nsec, nch), out_shape=(j...  50.5 us

profile of v10, /device:TPU:4, one launch (start us, length us, event | category | flops | bytes accessed | tf_op | source)
XLA Modules:
  0.0 53.5 jit_solution(14199722524206507265)
XLA Ops:
  0.6 50.5 %lanczos.1 = (f32[4,24,384]{2,1,0:T(8,128)S(1)}, f32[1,1]{1,0:T(1,128)}) custom-call(bf16[13,8,576]{2,1,0:T(8,128)(2,1)} %bitcast.13, bf16[13,8,576]{2,1,0:T(8,128)(2,1)} %bitcast.14, s32[1,128]{1,0:T(1,128)} %slot_in.1, f32[4,576]{1,0:T(4,128)} %bitcast.15, f32[4,24,384]{2,1,0:T(8,128)} %bitcast.12, bf16[13,256]{1,0:T(8,128)(2,1)} %bitcast.16, s32[1,4]{1,0:T(1,128)} %kept_in.1), custom_call_target="tpu_custom_call" | custom-call | tf_op jit(solution)/shard_map/lanczos/pallas_call | solution.py:487
  51.1 0.7 %copy.11 = f32[1,4,24,384]{3,2,1,0:T(8,128)} copy(f32[1,4,24,384]{3,2,1,0:T(8,128)S(1)} %bitcast.11) | data formatting | bytes 294912

commit v11 on v10

--- a/solution.py
+++ b/solution.py
@@ -166,14 +166,15 @@
     left_in, right_in, slot_in, tr_in, x_in, b_in, kept_in,
     out_ref, en_ref,
     left, right, slot_ref, tr, x_ref, b_ref, kept_ref, lsem,
-    wide, wire, cat, stage, recva, recvb, recvl, trecv, v_ref, st, strecv0, strecv1, vout,
-    tpad, tbd, ebd, b2, c2, c1, mixed, moved, acat,
+    wide, wire, cat, stage, recva, recvb, recvl, recvk, trecv, v_ref, st, strecv0, strecv1, vout,
+    tpad, tbd, ebd, b2, c2, c1, mixed, moved, early, acat,
     ssem, rsem, tssem, trsem, qssem, qrsem,
 ):
     me = lax.axis_index("sector")
     ch = lax.axis_index("chain")
     cap = left_in.shape[1]
-    recvs = (recva, recvb, recvl)
+    recvs = (recva, recvb, recvl, recvk)
+    parts = ((0, 0, 48, 0, 10), (0, 48, 16, 10, 3), (1, 0, 48, 0, 10), (1, 48, 16, 10, 3))
     my_z, my_y = me // NY, lax.rem(me, NY)
     nz = nsec // NY
 
@@ -197,8 +198,8 @@
     bar = pltpu.get_barrier_semaphore()
     loop(1, nsec, lambda j: pl.semaphore_signal(bar, inc=1, device_id=(ch, lax.rem(me + j, nsec)), device_id_type=MESH))
     loop(1, nch, lambda j: pl.semaphore_signal(bar, inc=1, device_id=(lax.rem(ch + j, nch), me), device_id_type=MESH))
-    def widen(src):
-        for w in range(NW):
+    def widen(src, first, n):
+        for w in range(first, first + n):
             row8 = src[w].astype(F)
             for c in range(4):
                 wide[c, cap * w:cap * w + cap, :] = row8[:, 128 * c:128 * c + 128]
@@ -214,10 +215,11 @@
             wire[s, row + 4 * n:row + 4 * n + half, :] = jnp.where(lane < 64, lo, 0.0)
             wire[s, row + 4 * n:row + 5 * n - half, :] = jnp.where(lane < 64, lo[0:n - half], hi)
 
-    def place(side, chosen):
-        cat[side] = wire[...].astype(H)
+    def place(part, chosen):
+        side, row, n = parts[part][:3]
+        cat[side, :, row:row + n] = wire[:, row:row + n, :].astype(H)
         for j in range(nsec):
-            stage[side, j] = cat[side, chosen[j]]
+            stage[side, j, row:row + n] = cat[side, chosen[j], row:row + n]
 
     def tcopy(j):
         return pltpu.make_async_remote_copy(
@@ -225,7 +227,8 @@
             device_id=(lax.rem(ch + j, nch), me), device_id_type=MESH)
 
     def ecopy(part, j):
-        src = stage.at[1, j] if part == 2 else stage.at[0, j, pl.ds(48 * part, 48 - 32 * part)]
+        side, row, n = parts[part][:3]
+        src = stage.at[side, j, pl.ds(row, n)]
         return pltpu.make_async_remote_copy(
             src_ref=src, dst_ref=recvs[part].at[j], send_sem=ssem.at[part], recv_sem=rsem.at[part],
             device_id=(ch, peer(j)), device_id_type=MESH)
@@ -247,27 +250,33 @@
         chosen.append(s)
     loads[1].wait()
     wire[...] = jnp.zeros_like(wire)
-    widen(left)
-    pack(1, 0, 0, NW)
-    place(1, chosen)
+    widen(left, 10, 3)
+    pack(1, 48, 10, 3)
+    place(3, chosen)
     pl.semaphore_wait(bar, nsec + nch - 2)
+    for j in order:
+        ecopy(3, j).start()
+    widen(left, 0, 10)
+    pack(1, 0, 0, 10)
+    place(2, chosen)
     for j in order:
         ecopy(2, j).start()
     loads[2].wait()
     trecv[ch] = tr[...]
     loop(1, nch, lambda j: tcopy(j).start())
     loads[3].wait()
-    widen(right)
+    widen(right, 0, NW)
     pack(0, 0, 0, 10)
-    pack(0, 48, 10, 3)
     place(0, chosen)
     for j in order:
         ecopy(0, j).start()
+    pack(0, 48, 10, 3)
+    place(1, chosen)
     for j in order:
         ecopy(1, j).start()
-    recvs[0][0] = stage[0, 0, 0:48]
-    recvs[1][0] = stage[0, 0, 48:64]
-    recvs[2][0] = stage[1, 0]
+    for part in range(4):
+        side, row, n = parts[part][:3]
+        recvs[part][0] = stage[side, 0, row:row + n]
     loads[4].wait()
     loads[5].wait()
     loads[6].wait()
@@ -349,21 +358,33 @@
             for i in range(n):
                 moved[w + i] = jnp.swapaxes(o[:, 128 * i:128 * i + 128].reshape(NB, NP, 128), 0, 1)
 
-    def left_step(k, a2, parts=2):
+    def columns(q, first, last):
+        return jnp.concatenate([jnp.concatenate([moved[w, q + j] for w in range(first, last)], 0) for j in range(2)], 1)
+
+    def emit(k, q, o):
+        for j in range(2):
+            oj = o[:, 128 * j:128 * j + 128]
+            y = jnp.where(tl == 0, oj[0:24], jnp.where(tl == 1, oj[24:48], jnp.where(tl == 2, oj[48:72], oj[72:96])))
+            v_ref[k + 1, pl.ds(q + j, NB, stride=NP), :] = y
+
+    def twice(a):
+        return jnp.concatenate([a, a], 1).astype(H)
+
+    def left_dot(a, r, both):
+        if both:
+            h = r.astype(H).astype(F)
+            r = jnp.concatenate([h, r - h], 0)
+        return jnp.dot(a, r.astype(H), preferred_element_type=F)
+
+    def left_step(k, a2, both):
+        a = a2 if both else a2[:, :24 * NW]
         for q in range(0, NP, 2):
-            r = jnp.concatenate([jnp.concatenate([moved[w, q + j] for w in range(NW)], 0) for j in range(2)], 1)
-            if parts == 2:
-                h = r.astype(H).astype(F)
-                r = jnp.concatenate([h, r - h], 0)
-            o = jnp.dot(a2[:, :312 * parts], r.astype(H), preferred_element_type=F)
-            for j in range(2):
-                oj = o[:, 128 * j:128 * j + 128]
-                y = jnp.where(tl == 0, oj[0:24], jnp.where(tl == 1, oj[24:48], jnp.where(tl == 2, oj[48:72], oj[72:96])))
-                v_ref[k + 1, pl.ds(q + j, NB, stride=NP), :] = y
+            emit(k, q, left_dot(a, columns(q, 0, NW), both))
 
     pair_step(0)
-    everyone(recvs[2], ssem.at[2], rsem.at[2]).wait()
-    spread(2, 0, NW)
+    for part in (3, 2):
+        everyone(recvs[part], ssem.at[part], rsem.at[part]).wait()
+        spread(part, *parts[part][3:])
     pp = jnp.concatenate([ph, plo], 0)
     pq = jnp.concatenate([ph, plo, ph], 0)
     for w in range(NW):
@@ -375,7 +396,7 @@
     acat[312:384, :] = jnp.zeros((72, 128), F)
     al = acat[...].T
     al = jnp.concatenate([al[32 * t:32 * t + 24] for t in range(NT)], 0)[:, :312].astype(H).astype(F)
-    a2 = jnp.concatenate([al, al], 1).astype(H)
+    a2 = twice(al)
     for part, first, last in ((0, 0, 10), (1, 10, NW)):
         everyone(recvs[part], ssem.at[part], rsem.at[part]).wait()
         spread(part, first, last - first)
@@ -386,6 +407,13 @@
             i = 128 * (w % 2)
             c1[w // 2, i:i + 128, i:i + 128] = ct
         right_step(first, last)
+        a = twice(al[:, 24 * first:24 * last])
+        for q in range(0, NP, 2):
+            o = left_dot(a, columns(q, first, last), True)
+            if part == 0:
+                early[q // 2] = o
+            else:
+                emit(0, q, early[q // 2] + o)
 
     alphas = []
     betas = []
@@ -393,7 +421,7 @@
         if k > 0:
             pair_step(k, 1)
             right_step_rounded()
-        left_step(k, a2, 2 if k < 2 else 1)
+            left_step(k, a2, k == 1)
         y = v_ref[k + 1]
         a = full(v_ref[k] * y)
         r = y - a * v_ref[k]
@@ -430,7 +458,7 @@
     strecv0[0] = s
     pair_step(3, 1)
     right_step_rounded()
-    left_step(3, a2, 1)
+    left_step(3, a2, False)
     s = jnp.zeros((1, 128), F)
     for i in range(4):
         s = s + jnp.where(lane == i, full(v_ref[i] * v_ref[4]), 0.0)
@@ -504,7 +532,8 @@
             pltpu.VMEM((2, nsec, 64, 128), H),
             pltpu.VMEM((nsec, 48, 128), H),
             pltpu.VMEM((nsec, 16, 128), H),
-            pltpu.VMEM((nsec, 64, 128), H),
+            pltpu.VMEM((nsec, 48, 128), H),
+            pltpu.VMEM((nsec, 16, 128), H),
             pltpu.VMEM((nch, NT, 576), F),
             pltpu.VMEM((5, 384, 128), F),
             pltpu.VMEM((2, 1, 128), F),
@@ -519,8 +548,9 @@
             pltpu.VMEM(((NW + 1) // 2, 256, 256), H),
             pltpu.VMEM((2, NB, 208, 128), H),
             pltpu.VMEM((NW, NP, NB, 128), F),
+            pltpu.VMEM((NP // 2, NT * NB, 256), F),
             pltpu.VMEM((384, 128), F),
-            dma((3,)), dma((3,)), dma((nch,)), dma((nch,)), dma((2,)), dma((2,)),
+            dma((4,)), dma((4,)), dma((nch,)), dma((nch,)), dma((2,)), dma((2,)),
         ],
         compiler_params=pltpu.CompilerParams(collective_id=0, has_side_effects=True, vmem_limit_bytes=48 * 2**20),
         name="lanczos",

time: 53.6 us -> 53.3 us (level)
  no operation moved by 1% of the time
where the time goes in v11:
time: 53.3 us; the launch traced here: 53.2 us
  Pallas kernels  50.2 us (94%)
  between operations  2.33 us (4%)
  local copies, waits for them, and re-layouts  0.66 us (1%)
    pallas_call x1, Pallas kernels, body(): pl.pallas_call(functools.partial(whole, entries, nsec, nch), out_shape=(j...  50.2 us

profile of v11, /device:TPU:4, one launch (start us, length us, event | category | flops | bytes accessed | tf_op | source)
XLA Modules:
  0.0 53.2 jit_solution(5947339890980078390)
XLA Ops:
  0.6 50.2 %lanczos.1 = (f32[4,24,384]{2,1,0:T(8,128)S(1)}, f32[1,1]{1,0:T(1,128)}) custom-call(bf16[13,8,576]{2,1,0:T(8,128)(2,1)} %bitcast.13, bf16[13,8,576]{2,1,0:T(8,128)(2,1)} %bitcast.14, s32[1,128]{1,0:T(1,128)} %slot_in.1, f32[4,576]{1,0:T(4,128)} %bitcast.15, f32[4,24,384]{2,1,0:T(8,128)} %bitcast.12, bf16[13,256]{1,0:T(8,128)(2,1)} %bitcast.16, s32[1,4]{1,0:T(1,128)} %kept_in.1), custom_call_target="tpu_custom_call" | custom-call | tf_op jit(solution)/shard_map/lanczos/pallas_call | solution.py:515
  50.8 0.7 %copy.11 = f32[1,4,24,384]{3,2,1,0:T(8,128)} copy(f32[1,4,24,384]{3,2,1,0:T(8,128)S(1)} %bitcast.11) | data formatting | bytes 294912

commit v12 on v11

--- a/solution.py
+++ b/solution.py
@@ -166,15 +166,15 @@
     left_in, right_in, slot_in, tr_in, x_in, b_in, kept_in,
     out_ref, en_ref,
     left, right, slot_ref, tr, x_ref, b_ref, kept_ref, lsem,
-    wide, wire, cat, stage, recva, recvb, recvl, recvk, trecv, v_ref, st, strecv0, strecv1, vout,
+    wide, wire, cat, stage, recva, recvb, recvl, trecv, v_ref, st, strecv0, strecv1, vout,
     tpad, tbd, ebd, b2, c2, c1, mixed, moved, early, acat,
     ssem, rsem, tssem, trsem, qssem, qrsem,
 ):
     me = lax.axis_index("sector")
     ch = lax.axis_index("chain")
     cap = left_in.shape[1]
-    recvs = (recva, recvb, recvl, recvk)
-    parts = ((0, 0, 48, 0, 10), (0, 48, 16, 10, 3), (1, 0, 48, 0, 10), (1, 48, 16, 10, 3))
+    recvs = (recva, recvb, recvl)
+    parts = ((0, 0, 48, 0, 10), (0, 48, 16, 10, 3), (1, 0, 64, 0, NW))
     my_z, my_y = me // NY, lax.rem(me, NY)
     nz = nsec // NY
 
@@ -250,15 +250,10 @@
         chosen.append(s)
     loads[1].wait()
     wire[...] = jnp.zeros_like(wire)
-    widen(left, 10, 3)
-    pack(1, 48, 10, 3)
-    place(3, chosen)
+    widen(left, 0, NW)
+    pack(1, 0, 0, NW)
+    place(2, chosen)
     pl.semaphore_wait(bar, nsec + nch - 2)
-    for j in order:
-        ecopy(3, j).start()
-    widen(left, 0, 10)
-    pack(1, 0, 0, 10)
-    place(2, chosen)
     for j in order:
         ecopy(2, j).start()
     loads[2].wait()
@@ -274,7 +269,7 @@
     place(1, chosen)
     for j in order:
         ecopy(1, j).start()
-    for part in range(4):
+    for part in range(3):
         side, row, n = parts[part][:3]
         recvs[part][0] = stage[side, 0, row:row + n]
     loads[4].wait()
@@ -382,9 +377,8 @@
             emit(k, q, left_dot(a, columns(q, 0, NW), both))
 
     pair_step(0)
-    for part in (3, 2):
-        everyone(recvs[part], ssem.at[part], rsem.at[part]).wait()
-        spread(part, *parts[part][3:])
+    everyone(recvs[2], ssem.at[2], rsem.at[2]).wait()
+    spread(2, 0, NW)
     pp = jnp.concatenate([ph, plo], 0)
     pq = jnp.concatenate([ph, plo, ph], 0)
     for w in range(NW):
@@ -427,10 +421,11 @@
         r = y - a * v_ref[k]
         if k > 0:
             r = r - betas[-1] * v_ref[k - 1]
-        b = jnp.sqrt(full(r * r))
+        rr = full(r * r)
+        b = jnp.sqrt(rr)
         alphas.append(a)
         betas.append(b)
-        v_ref[k + 1] = r * inverse(b)
+        v_ref[k + 1] = r * jnp.where(rr > 0, lax.rsqrt(rr), 0.0)
 
     def qcopy(i, j):
         return pltpu.make_async_remote_copy(
@@ -532,8 +527,7 @@
             pltpu.VMEM((2, nsec, 64, 128), H),
             pltpu.VMEM((nsec, 48, 128), H),
             pltpu.VMEM((nsec, 16, 128), H),
-            pltpu.VMEM((nsec, 48, 128), H),
-            pltpu.VMEM((nsec, 16, 128), H),
+            pltpu.VMEM((nsec, 64, 128), H),
             pltpu.VMEM((nch, NT, 576), F),
             pltpu.VMEM((5, 384, 128), F),
             pltpu.VMEM((2, 1, 128), F),
@@ -550,7 +544,7 @@
             pltpu.VMEM((NW, NP, NB, 128), F),
             pltpu.VMEM((NP // 2, NT * NB, 256), F),
             pltpu.VMEM((384, 128), F),
-            dma((4,)), dma((4,)), dma((nch,)), dma((nch,)), dma((2,)), dma((2,)),
+            dma((3,)), dma((3,)), dma((nch,)), dma((nch,)), dma((2,)), dma((2,)),
         ],
         compiler_params=pltpu.CompilerParams(collective_id=0, has_side_effects=True, vmem_limit_bytes=48 * 2**20),
         name="lanczos",

time: 53.3 us -> 53.2 us (level)
  no operation moved by 1% of the time
where the time goes in v12:
time: 53.2 us; the launch traced here: 53.1 us
  Pallas kernels  50.1 us (94%)
  between operations  2.33 us (4%)
  local copies, waits for them, and re-layouts  0.66 us (1%)
    pallas_call x1, Pallas kernels, body(): pl.pallas_call(functools.partial(whole, entries, nsec, nch), out_shape=(j...  50.1 us

profile of v12, /device:TPU:4, one launch (start us, length us, event | category | flops | bytes accessed | tf_op | source)
XLA Modules:
  0.0 53.1 jit_solution(7134486637026676473)
XLA Ops:
  0.6 50.1 %lanczos.1 = (f32[4,24,384]{2,1,0:T(8,128)S(1)}, f32[1,1]{1,0:T(1,128)}) custom-call(bf16[13,8,576]{2,1,0:T(8,128)(2,1)} %bitcast.13, bf16[13,8,576]{2,1,0:T(8,128)(2,1)} %bitcast.14, s32[1,128]{1,0:T(1,128)} %slot_in.1, f32[4,576]{1,0:T(4,128)} %bitcast.15, f32[4,24,384]{2,1,0:T(8,128)} %bitcast.12, bf16[13,256]{1,0:T(8,128)(2,1)} %bitcast.16, s32[1,4]{1,0:T(1,128)} %kept_in.1), custom_call_target="tpu_custom_call" | custom-call | tf_op jit(solution)/shard_map/lanczos/pallas_call | solution.py:510
  50.7 0.7 %copy.11 = f32[1,4,24,384]{3,2,1,0:T(8,128)} copy(f32[1,4,24,384]{3,2,1,0:T(8,128)S(1)} %bitcast.11) | data formatting | bytes 294912

commit v13 on v12

--- a/solution.py
+++ b/solution.py
@@ -141,7 +141,7 @@
         lo = jnp.max(jnp.max(x, axis=0, keepdims=True), axis=1, keepdims=True)
         hi = lo + h
     e = lo
-    for _ in range(3):
+    for _ in range(2):
         vp, vn, sp, sn = jnp.ones_like(e), d[0] - e, jnp.zeros_like(e), -jnp.ones_like(e)
         for p in range(1, 4):
             z = d[p] - e
@@ -196,8 +196,11 @@
     for c in loads:
         c.start()
     bar = pltpu.get_barrier_semaphore()
-    loop(1, nsec, lambda j: pl.semaphore_signal(bar, inc=1, device_id=(ch, lax.rem(me + j, nsec)), device_id_type=MESH))
-    loop(1, nch, lambda j: pl.semaphore_signal(bar, inc=1, device_id=(lax.rem(ch + j, nch), me), device_id_type=MESH))
+    for j in far:
+        pl.semaphore_signal(bar, inc=1, device_id=(ch, peer(j)), device_id_type=MESH)
+    for j in range(1, nch):
+        pl.semaphore_signal(bar, inc=1, device_id=(lax.rem(ch + j, nch), me), device_id_type=MESH)
+
     def widen(src, first, n):
         for w in range(first, first + n):
             row8 = src[w].astype(F)
@@ -258,7 +261,8 @@
         ecopy(2, j).start()
     loads[2].wait()
     trecv[ch] = tr[...]
-    loop(1, nch, lambda j: tcopy(j).start())
+    for j in range(1, nch):
+        tcopy(j).start()
     loads[3].wait()
     widen(right, 0, NW)
     pack(0, 0, 0, 10)

time: 53.2 us -> 53 us (level)
  no operation moved by 1% of the time
where the time goes in v13:
time: 53 us; the launch traced here: 52.9 us
  Pallas kernels  49.9 us (94%)
  between operations  2.33 us (4%)
  local copies, waits for them, and re-layouts  0.66 us (1%)
    pallas_call x1, Pallas kernels, body(): pl.pallas_call(functools.partial(whole, entries, nsec, nch), out_shape=(j...  49.9 us

profile of v13, /device:TPU:4, one launch (start us, length us, event | category | flops | bytes accessed | tf_op | source)
XLA Modules:
  0.0 52.9 jit_solution(1237661335980632084)
XLA Ops:
  0.6 49.9 %lanczos.1 = (f32[4,24,384]{2,1,0:T(8,128)S(1)}, f32[1,1]{1,0:T(1,128)}) custom-call(bf16[13,8,576]{2,1,0:T(8,128)(2,1)} %bitcast.13, bf16[13,8,576]{2,1,0:T(8,128)(2,1)} %bitcast.14, s32[1,128]{1,0:T(1,128)} %slot_in.1, f32[4,576]{1,0:T(4,128)} %bitcast.15, f32[4,24,384]{2,1,0:T(8,128)} %bitcast.12, bf16[13,256]{1,0:T(8,128)(2,1)} %bitcast.16, s32[1,4]{1,0:T(1,128)} %kept_in.1), custom_call_target="tpu_custom_call" | custom-call | tf_op jit(solution)/shard_map/lanczos/pallas_call | solution.py:514
  50.6 0.7 %copy.11 = f32[1,4,24,384]{3,2,1,0:T(8,128)} copy(f32[1,4,24,384]{3,2,1,0:T(8,128)S(1)} %bitcast.11) | data formatting | bytes 294912

commit v14 on v13

--- a/solution.py
+++ b/solution.py
@@ -220,7 +220,7 @@
 
     def place(part, chosen):
         side, row, n = parts[part][:3]
-        cat[side, :, row:row + n] = wire[:, row:row + n, :].astype(H)
+        cat[side, :, row:row + n] = wire[0:cap, row:row + n, :].astype(H)
         for j in range(nsec):
             stage[side, j, row:row + n] = cat[side, chosen[j], row:row + n]
 
@@ -525,8 +525,8 @@
             pltpu.VMEM(pair_ops.shape[1:], H),
             pltpu.SMEM(kept_ranks.shape, jnp.int32),
             dma((7,)),
-            pltpu.VMEM((5, cap * NW, 128), F),
-            pltpu.VMEM((cap, 64, 128), F),
+            pltpu.VMEM((5, cap * 20, 128), F),
+            pltpu.VMEM((cap + 1, 64, 128), F),
             pltpu.VMEM((2, cap, 64, 128), H),
             pltpu.VMEM((2, nsec, 64, 128), H),
             pltpu.VMEM((nsec, 48, 128), H),
@@ -540,7 +540,7 @@
             pltpu.VMEM((3, NT, NB, NP * NB), F),
             pltpu.VMEM((16, 640), F),
             pltpu.VMEM((1024, 128), F),
-            pltpu.VMEM((1664, 128), F),
+            pltpu.VMEM((2304, 128), F),
             pltpu.VMEM((208, 32), H),
             pltpu.VMEM((NW, 256, 128), H),
             pltpu.VMEM(((NW + 1) // 2, 256, 256), H),

time: 53 us -> 53 us (level)
  no operation moved by 1% of the time
where the time goes in v14:
time: 53 us; the launch traced here: 52.9 us
  Pallas kernels  49.9 us (94%)
  between operations  2.33 us (4%)
  local copies, waits for them, and re-layouts  0.66 us (1%)
    pallas_call x1, Pallas kernels, body(): pl.pallas_call(functools.partial(whole, entries, nsec, nch), out_shape=(j...  49.9 us

profile of v14, /device:TPU:4, one launch (start us, length us, event | category | flops | bytes accessed | tf_op | source)
XLA Modules:
  0.0 52.9 jit_solution(10669770592476297059)
XLA Ops:
  0.6 49.9 %lanczos.1 = (f32[4,24,384]{2,1,0:T(8,128)S(1)}, f32[1,1]{1,0:T(1,128)}) custom-call(bf16[13,8,576]{2,1,0:T(8,128)(2,1)} %bitcast.13, bf16[13,8,576]{2,1,0:T(8,128)(2,1)} %bitcast.14, s32[1,128]{1,0:T(1,128)} %slot_in.1, f32[4,576]{1,0:T(4,128)} %bitcast.15, f32[4,24,384]{2,1,0:T(8,128)} %bitcast.12, bf16[13,256]{1,0:T(8,128)(2,1)} %bitcast.16, s32[1,4]{1,0:T(1,128)} %kept_in.1), custom_call_target="tpu_custom_call" | custom-call | tf_op jit(solution)/shard_map/lanczos/pallas_call | solution.py:514
  50.6 0.7 %copy.11 = f32[1,4,24,384]{3,2,1,0:T(8,128)} copy(f32[1,4,24,384]{3,2,1,0:T(8,128)S(1)} %bitcast.11) | data formatting | bytes 294912
